TPU v7x, 32 devices: a whole 2x2x4 slice. The times are simulated.
32 devices in a mesh: grp: 2 (over y), bl: 4 (over z), ch: 2 (over x), pol: 2 (over core).
Axes of the slice: x: 2, y: 2, z: 4, core: 2. Of those that a mesh axis runs over, the one named last changes fastest.
Arguments:
- visibilities: float32 [2, 2, 256, 2048], P(None, 'pol', 'ch', ('grp', 'bl')), parts along dimension 3
- beam: float32 [16, 2, 2, 256, 512], P('grp', None, 'pol', 'ch', 'bl'), parts along dimension 0, may hold values from -1.4 to 1.4, as said below
- coherency: float32 [16, 2, 256], P(('grp', 'bl'), 'pol', 'ch'), parts along dimension 0, may hold values from 0.5 to 3, as said below
- owner: int32 [16], P('grp'), parts along dimension 0, may hold values from 0 to 7, as said below
- positions: float32 [2, 1024], P(None, 'grp'), parts along dimension 1, may hold values from -2 to 2
- direction_lm: float32 [16, 2], P('grp'), parts along dimension 0, may hold values from -0.3 to 0.3
- pairs: int32 [2, 2048], P(None, ('grp', 'bl')), parts along dimension 1, may hold values from 0 to 511, as said below
Outputs:
- residual: float32 [2, 2, 256, 2048], P(None, 'pol', 'ch', ('grp', 'bl')), parts along dimension 3
- gains: float32 [16, 2, 2, 512], P('grp', None, 'pol'), parts along dimension 0
There are 2 independent parts, one for each index of `grp`. A program takes and returns all parts, laid end to end along the dimension named above; each array names one. Nothing has to cross between parts.
Inputs may be any that keep to these rules, and one draw needn't show every extreme that they name: `pairs`: each device's 2 * 128 baseline slots hold whole tiles of live baselines first, then padding; a live slot names two different stations, the first below the second; a padding slot names station 0 twice; every device has at least one live tile and some device has all slots live. `owner`: 8 different rows of the coherency table; row k is held by index k // 2 of bl. Positive coherency spectra. `beam`: beam Jones magnitudes between 0.6 and 1.4.
All inputs are finite; a program needn't handle non-finite values.
Results may differ from a plain program's by a relative error of at most 0.0001.
Values sent between devices are 32-bit elements; how exact they have to be, the bound alone decides.
A program may use at most 128 MiB of HBM per device.

v0:
```python
import math

import jax
import jax.numpy as jnp
from jax import lax
from jax.sharding import PartitionSpec as P

NC = 256
DIRS = 8
ITERS = 2


MIXING = 0.5


def from_root(value, axis, source):
    kept = jnp.where(lax.axis_index(axis) == source, value, 0).astype(value.dtype)
    return lax.psum(kept, axis)


def predict(beam_dir, flux_row, first, second, east_diff, north_diff, lm_dir, freq, live):
    left_r = beam_dir[0][:, :, first]
    left_i = beam_dir[1][:, :, first]
    right_r = beam_dir[0][:, :, second]
    right_i = beam_dir[1][:, :, second]
    cross_r = left_r * right_r + left_i * right_i
    cross_i = left_i * right_r - left_r * right_i
    phase = (
        2.0 * math.pi * freq[:, None] * (east_diff * lm_dir[0] + north_diff * lm_dir[1])[None, :]
    )
    cosine = jnp.cos(phase)
    sine = jnp.sin(phase)
    scale = flux_row[:, :, None] * live[None, None, :]
    model_r = (cross_r * cosine - cross_i * sine) * scale
    model_i = (cross_r * sine + cross_i * cosine) * scale
    return (model_r, model_i)


def slot_products(res_r, res_i, model_r, model_i):
    prod_r = jnp.sum(res_r * model_r + res_i * model_i, axis=1)
    prod_i = jnp.sum(res_i * model_r - res_r * model_i, axis=1)
    power = jnp.sum(model_r * model_r + model_i * model_i, axis=1)
    return (prod_r, prod_i, power)


def segsum(values, index, stations):
    return jax.ops.segment_sum(values.T, index, stations).T


def weight_of(power, first, second, stations):
    return segsum(power, first, stations) + segsum(power, second, stations)


def gain_sums(prod_r, prod_i, power, gain_r, gain_i, first, second, stations):
    far_r = gain_r[:, second]
    far_i = gain_i[:, second]
    near_r = gain_r[:, first]
    near_i = gain_i[:, first]
    head_r = prod_r * far_r - prod_i * far_i
    head_i = prod_r * far_i + prod_i * far_r
    tail_r = prod_r * near_r + prod_i * near_i
    tail_i = prod_r * near_i - prod_i * near_r
    den_head = power * (far_r * far_r + far_i * far_i)
    den_tail = power * (near_r * near_r + near_i * near_i)
    return jnp.stack(
        [
            segsum(head_r, first, stations) + segsum(tail_r, second, stations),
            segsum(head_i, first, stations) + segsum(tail_i, second, stations),
            segsum(den_head, first, stations) + segsum(den_tail, second, stations),
        ]
    )


def update_gains(sums, weight, gain_r, gain_i):
    top_r = sums[0] + MIXING * weight + 1.0
    top_i = sums[1]
    bottom = sums[2] + MIXING * weight + 1.0
    return (0.5 * gain_r + 0.5 * top_r / bottom, 0.5 * gain_i + 0.5 * top_i / bottom)


def subtract(res_r, res_i, model_r, model_i, gain_r, gain_i, first, second):
    near_r = gain_r[:, first]
    near_i = gain_i[:, first]
    far_r = gain_r[:, second]
    far_i = gain_i[:, second]
    pair_r = (near_r * far_r + near_i * far_i)[:, None, :]
    pair_i = (near_i * far_r - near_r * far_i)[:, None, :]
    res_r = res_r - (pair_r * model_r - pair_i * model_i)
    res_i = res_i - (pair_r * model_i + pair_i * model_r)
    return (res_r, res_i)


def on_device(visibilities, beam, coherency, owner, positions, direction_lm, pairs):
    first = pairs[0]
    second = pairs[1]
    live = (first != second).astype(jnp.float32)
    chan_count = visibilities.shape[2]
    channel = lax.axis_index("ch") * chan_count + jnp.arange(chan_count)
    freq = 1.0 + 0.5 * channel.astype(jnp.float32) / NC
    east_diff = positions[0, first] - positions[0, second]
    north_diff = positions[1, first] - positions[1, second]
    stations = positions.shape[1]
    slot_dev = coherency.shape[0]
    res_r = visibilities[0]
    res_i = visibilities[1]
    solved = []
    for direction in range(DIRS):
        beam_dir = lax.all_gather(beam[direction], "bl", axis=3, tiled=True)
        local_row = lax.dynamic_index_in_dim(
            coherency, owner[direction] % slot_dev, 0, keepdims=False
        )
        flux_row = from_root(local_row, "bl", owner[direction] // slot_dev)
        model_r, model_i = predict(
            beam_dir,
            flux_row,
            first,
            second,
            east_diff,
            north_diff,
            direction_lm[direction],
            freq,
            live,
        )
        prod_r, prod_i, power = slot_products(res_r, res_i, model_r, model_i)
        gain_r = jnp.ones((res_r.shape[0], stations), jnp.float32)
        gain_i = jnp.zeros((res_r.shape[0], stations), jnp.float32)
        weight = lax.psum(weight_of(power, first, second, stations), ("bl", "ch"))
        for sweep in range(ITERS):
            partial_value = gain_sums(
                prod_r, prod_i, power, gain_r, gain_i, first, second, stations
            )
            totals = lax.psum(partial_value, ("bl", "ch"))
            gain_r, gain_i = update_gains(totals, weight, gain_r, gain_i)
        res_r, res_i = subtract(res_r, res_i, model_r, model_i, gain_r, gain_i, first, second)
        solved.append(jnp.stack([gain_r, gain_i]))
    return (jnp.stack([res_r, res_i]), jnp.stack(solved))


def solution(mesh):
    return jax.shard_map(
        on_device,
        mesh=mesh,
        in_specs=(
            P(None, "pol", "ch", ("grp", "bl")),
            P("grp", None, "pol", "ch", "bl"),
            P(("grp", "bl"), "pol", "ch"),
            P("grp"),
            P(None, "grp"),
            P("grp", None),
            P(None, ("grp", "bl")),
        ),
        out_specs=(P(None, "pol", "ch", ("grp", "bl")), P("grp", None, "pol", None)),
        check_vma=False,
    )
```

profile of v0, /device:TPU:0, one launch (start us, length us, event | category | flops | bytes accessed | tf_op | source)
XLA Modules:
  0.0 947.4 jit_solution(9698187927695877635)
XLA Ops:
  24.4 14.0 %all-reduce.12 = (f32[128]{0:T(128)S(1)}, f32[128]{0:T(128)S(1)}, f32[128]{0:T(128)S(1)}, f32[128]{0:T(128)S(1)}, f32[128]{0:T(128)S(1)}, /*index=5*/f32[128]{0:T(128)}, f32[128]{0:T(128)}, f32[128]{0:T(128)S(1)}) all-reduce(f32[128]{0:T(128)S(1)} %get-tuple-element.355, ...), channel_id=1, replica_groups=mesh['grp'=2,'bl'=4,'ch'=2,'pol'=2] {'bl'}, use_global_device_ids=true, to_apply=%region_0.1 | all-reduce | flops 1024 | bytes 8192 | tf_op jit(solution)/shard_map/psum | solution.py:18
  39.8 2.5 gather_fusion.4
  42.3 2.5 gather_fusion.5
  44.9 2.5 gather_fusion.6
  47.4 2.5 gather_fusion.7
  52.1 14.8 %all-gather.7 = f32[1,2,1,128,512]{3,4,2,1,0:T(8,128)S(1)} all-gather(f32[1,2,1,128,128]{3,4,2,1,0:T(8,128)S(1)} %copy.40), channel_id=9, replica_groups=mesh['grp'=2,'bl'=4,'ch'=2,'pol'=2] {'bl'}, dimensions={4}, use_global_device_ids=true | all-gather | bytes 655360 | tf_op jit(solution)/shard_map/all_gather | solution.py:108
  69.9 15.5 %all-gather = f32[1,2,1,128,512]{3,4,2,1,0:T(8,128)S(1)} all-gather(f32[1,2,1,128,128]{3,4,2,1,0:T(8,128)S(1)} %copy.32), channel_id=2, replica_groups=mesh['grp'=2,'bl'=4,'ch'=2,'pol'=2] {'bl'}, dimensions={4}, use_global_device_ids=true | all-gather | bytes 655360 | tf_op jit(solution)/shard_map/all_gather | solution.py:108
  88.4 8.6 multiply_add_fusion.51
  112.1 2.5 scatter_custom_fusion.2
  126.2 19.6 %all-reduce.11 = (f32[3,1,512]{2,1,0:T(1,128)S(1)}, f32[1,512]{1,0:T(1,128)S(1)}) all-reduce(f32[3,1,512]{2,1,0:T(1,128)S(1)} %pad_maximum_fusion.1, f32[1,512]{1,0:T(1,128)S(1)} %bitcast.1040), channel_id=1, replica_groups=mesh['grp'=2,'bl'=4,'ch'=2,'pol'=2] {'bl','ch'}, use_global_device_ids=true, to_apply=%region_10.11 | all-reduce | flops 2048 | bytes 16384 | tf_op jit(solution)/shard_map/psum | solution.py:132
  156.0 2.7 scatter_custom_fusion.13
  168.1 17.6 %psum.244 = f32[3,1,512]{2,1,0:T(1,128)S(1)} all-reduce(f32[3,1,512]{2,1,0:T(1,128)S(1)} %pad_maximum_fusion.2), channel_id=1, replica_groups=mesh['grp'=2,'bl'=4,'ch'=2,'pol'=2] {'bl','ch'}, use_global_device_ids=true, to_apply=%region_20.21 | all-reduce | flops 1536 | bytes 12288 | tf_op jit(solution)/shard_map/psum | solution.py:132
  193.6 14.7 %all-gather.1 = f32[1,2,1,128,512]{3,4,2,1,0:T(8,128)S(1)} all-gather(f32[1,2,1,128,128]{3,4,2,1,0:T(8,128)S(1)} %copy.34), channel_id=3, replica_groups=mesh['grp'=2,'bl'=4,'ch'=2,'pol'=2] {'bl'}, dimensions={4}, use_global_device_ids=true | all-gather | bytes 655360 | tf_op jit(solution)/shard_map/all_gather | solution.py:108
  212.1 2.5 scatter_custom_fusion.18
  214.6 2.6 scatter_custom_fusion.19
  217.2 2.5 scatter_custom_fusion.16
  222.1 2.5 scatter_custom_fusion.14
  227.1 2.5 scatter_custom_fusion.20
  232.0 19.5 %all-reduce.10 = (f32[3,1,512]{2,1,0:T(1,128)S(1)}, f32[1,512]{1,0:T(1,128)S(1)}) all-reduce(f32[3,1,512]{2,1,0:T(1,128)S(1)} %pad_maximum_fusion.3, f32[1,512]{1,0:T(1,128)S(1)} %bitcast.1041), channel_id=1, replica_groups=mesh['grp'=2,'bl'=4,'ch'=2,'pol'=2] {'bl','ch'}, use_global_device_ids=true, to_apply=%region_31.32 | all-reduce | flops 2048 | bytes 16384 | tf_op jit(solution)/shard_map/psum | solution.py:132
  259.4 2.7 scatter_custom_fusion.26
  262.0 2.5 scatter_custom_fusion.27
  264.5 2.5 scatter_custom_fusion.24
  269.4 2.5 scatter_custom_fusion.22
  274.3 17.5 %psum.249 = f32[3,1,512]{2,1,0:T(1,128)S(1)} all-reduce(f32[3,1,512]{2,1,0:T(1,128)S(1)} %pad_maximum_fusion.4), channel_id=1, replica_groups=mesh['grp'=2,'bl'=4,'ch'=2,'pol'=2] {'bl','ch'}, use_global_device_ids=true, to_apply=%region_41.42 | all-reduce | flops 1536 | bytes 12288 | tf_op jit(solution)/shard_map/psum | solution.py:132
  299.8 14.7 %all-gather.2 = f32[1,2,1,128,512]{3,4,2,1,0:T(8,128)S(1)} all-gather(f32[1,2,1,128,128]{3,4,2,1,0:T(8,128)S(1)} %copy.35), channel_id=4, replica_groups=mesh['grp'=2,'bl'=4,'ch'=2,'pol'=2] {'bl'}, dimensions={4}, use_global_device_ids=true | all-gather | bytes 655360 | tf_op jit(solution)/shard_map/all_gather | solution.py:108
  319.5 2.8 scatter_custom_fusion.32
  322.4 2.5 scatter_custom_fusion.33
  324.9 2.5 scatter_custom_fusion.30
  329.8 2.5 scatter_custom_fusion.28
  334.7 2.5 scatter_custom_fusion.34
  339.6 19.9 %all-reduce.9 = (f32[3,1,512]{2,1,0:T(1,128)S(1)}, f32[1,512]{1,0:T(1,128)S(1)}) all-reduce(f32[3,1,512]{2,1,0:T(1,128)S(1)} %pad_maximum_fusion.5, f32[1,512]{1,0:T(1,128)S(1)} %bitcast.1042), channel_id=1, replica_groups=mesh['grp'=2,'bl'=4,'ch'=2,'pol'=2] {'bl','ch'}, use_global_device_ids=true, to_apply=%region_52.53 | all-reduce | flops 2048 | bytes 16384 | tf_op jit(solution)/shard_map/psum | solution.py:132
  367.3 2.5 scatter_custom_fusion.40
  372.2 2.5 scatter_custom_fusion.38
  377.2 2.5 scatter_custom_fusion.36
  382.1 17.4 %psum.254 = f32[3,1,512]{2,1,0:T(1,128)S(1)} all-reduce(f32[3,1,512]{2,1,0:T(1,128)S(1)} %pad_maximum_fusion.6), channel_id=1, replica_groups=mesh['grp'=2,'bl'=4,'ch'=2,'pol'=2] {'bl','ch'}, use_global_device_ids=true, to_apply=%region_62.63 | all-reduce | flops 1536 | bytes 12288 | tf_op jit(solution)/shard_map/psum | solution.py:132
  407.4 15.1 %all-gather.3 = f32[1,2,1,128,512]{3,4,2,1,0:T(8,128)S(1)} all-gather(f32[1,2,1,128,128]{3,4,2,1,0:T(8,128)S(1)} %copy.36), channel_id=5, replica_groups=mesh['grp'=2,'bl'=4,'ch'=2,'pol'=2] {'bl'}, dimensions={4}, use_global_device_ids=true | all-gather | bytes 655360 | tf_op jit(solution)/shard_map/all_gather | solution.py:108
  426.3 2.5 scatter_custom_fusion.46
  431.2 2.5 scatter_custom_fusion.44
  436.1 2.5 scatter_custom_fusion.42
  441.1 2.8 scatter_custom_fusion.48
  446.4 19.6 %all-reduce.8 = (f32[3,1,512]{2,1,0:T(1,128)S(1)}, f32[1,512]{1,0:T(1,128)S(1)}) all-reduce(f32[3,1,512]{2,1,0:T(1,128)S(1)} %pad_maximum_fusion.7, f32[1,512]{1,0:T(1,128)S(1)} %bitcast.1043), channel_id=1, replica_groups=mesh['grp'=2,'bl'=4,'ch'=2,'pol'=2] {'bl','ch'}, use_global_device_ids=true, to_apply=%region_73.74 | all-reduce | flops 2048 | bytes 16384 | tf_op jit(solution)/shard_map/psum | solution.py:132
  488.6 17.5 %psum.259 = f32[3,1,512]{2,1,0:T(1,128)S(1)} all-reduce(f32[3,1,512]{2,1,0:T(1,128)S(1)} %pad_maximum_fusion.8), channel_id=1, replica_groups=mesh['grp'=2,'bl'=4,'ch'=2,'pol'=2] {'bl','ch'}, use_global_device_ids=true, to_apply=%region_83.84 | all-reduce | flops 1536 | bytes 12288 | tf_op jit(solution)/shard_map/psum | solution.py:132
  514.1 14.7 %all-gather.4 = f32[1,2,1,128,512]{3,4,2,1,0:T(8,128)S(1)} all-gather(f32[1,2,1,128,128]{3,4,2,1,0:T(8,128)S(1)} %copy.37), channel_id=6, replica_groups=mesh['grp'=2,'bl'=4,'ch'=2,'pol'=2] {'bl'}, dimensions={4}, use_global_device_ids=true | all-gather | bytes 655360 | tf_op jit(solution)/shard_map/all_gather | solution.py:108
  545.5 2.6 scatter_custom_fusion.57
  553.1 19.7 %all-reduce.7 = (f32[3,1,512]{2,1,0:T(1,128)S(1)}, f32[1,512]{1,0:T(1,128)S(1)}) all-reduce(f32[3,1,512]{2,1,0:T(1,128)S(1)} %pad_maximum_fusion.9, f32[1,512]{1,0:T(1,128)S(1)} %bitcast.1044), channel_id=1, replica_groups=mesh['grp'=2,'bl'=4,'ch'=2,'pol'=2] {'bl','ch'}, use_global_device_ids=true, to_apply=%region_94.95 | all-reduce | flops 2048 | bytes 16384 | tf_op jit(solution)/shard_map/psum | solution.py:132
  590.5 2.8 scatter_custom_fusion.64
  595.8 17.4 %psum.264 = f32[3,1,512]{2,1,0:T(1,128)S(1)} all-reduce(f32[3,1,512]{2,1,0:T(1,128)S(1)} %pad_maximum_fusion.10), channel_id=1, replica_groups=mesh['grp'=2,'bl'=4,'ch'=2,'pol'=2] {'bl','ch'}, use_global_device_ids=true, to_apply=%region_104.105 | all-reduce | flops 1536 | bytes 12288 | tf_op jit(solution)/shard_map/psum | solution.py:132
  621.7 14.7 %all-gather.5 = f32[1,2,1,128,512]{3,4,2,1,0:T(8,128)S(1)} all-gather(f32[1,2,1,128,128]{3,4,2,1,0:T(8,128)S(1)} %copy.38), channel_id=7, replica_groups=mesh['grp'=2,'bl'=4,'ch'=2,'pol'=2] {'bl'}, dimensions={4}, use_global_device_ids=true | all-gather | bytes 655360 | tf_op jit(solution)/shard_map/all_gather | solution.py:108
  654.6 2.6 scatter_custom_fusion.70
  665.3 19.8 %all-reduce.6 = (f32[3,1,512]{2,1,0:T(1,128)S(1)}, f32[1,512]{1,0:T(1,128)S(1)}) all-reduce(f32[3,1,512]{2,1,0:T(1,128)S(1)} %pad_maximum_fusion.11, f32[1,512]{1,0:T(1,128)S(1)} %bitcast.1045), channel_id=1, replica_groups=mesh['grp'=2,'bl'=4,'ch'=2,'pol'=2] {'bl','ch'}, use_global_device_ids=true, to_apply=%region_115.116 | all-reduce | flops 2048 | bytes 16384 | tf_op jit(solution)/shard_map/psum | solution.py:132
  700.4 2.6 scatter_custom_fusion.81
  708.0 17.4 %psum.269 = f32[3,1,512]{2,1,0:T(1,128)S(1)} all-reduce(f32[3,1,512]{2,1,0:T(1,128)S(1)} %pad_maximum_fusion.12), channel_id=1, replica_groups=mesh['grp'=2,'bl'=4,'ch'=2,'pol'=2] {'bl','ch'}, use_global_device_ids=true, to_apply=%region_125.126 | all-reduce | flops 1536 | bytes 12288 | tf_op jit(solution)/shard_map/psum | solution.py:132
  733.9 14.7 %all-gather.6 = f32[1,2,1,128,512]{3,4,2,1,0:T(8,128)S(1)} all-gather(f32[1,2,1,128,128]{3,4,2,1,0:T(8,128)S(1)} %copy.39), channel_id=8, replica_groups=mesh['grp'=2,'bl'=4,'ch'=2,'pol'=2] {'bl'}, dimensions={4}, use_global_device_ids=true | all-gather | bytes 655360 | tf_op jit(solution)/shard_map/all_gather | solution.py:108
  754.1 3.0 add_reduce_fusion.3
  765.7 2.8 scatter_custom_fusion.87
  779.0 19.7 %all-reduce.5 = (f32[3,1,512]{2,1,0:T(1,128)S(1)}, f32[1,512]{1,0:T(1,128)S(1)}) all-reduce(f32[3,1,512]{2,1,0:T(1,128)S(1)} %pad_maximum_fusion.13, f32[1,512]{1,0:T(1,128)S(1)} %bitcast.1046), channel_id=1, replica_groups=mesh['grp'=2,'bl'=4,'ch'=2,'pol'=2] {'bl','ch'}, use_global_device_ids=true, to_apply=%region_136.137 | all-reduce | flops 2048 | bytes 16384 | tf_op jit(solution)/shard_map/psum | solution.py:132
  811.6 2.6 scatter_custom_fusion.94
  821.6 17.4 %psum.274 = f32[3,1,512]{2,1,0:T(1,128)S(1)} all-reduce(f32[3,1,512]{2,1,0:T(1,128)S(1)} %pad_maximum_fusion.14), channel_id=1, replica_groups=mesh['grp'=2,'bl'=4,'ch'=2,'pol'=2] {'bl','ch'}, use_global_device_ids=true, to_apply=%region_146.147 | all-reduce | flops 1536 | bytes 12288 | tf_op jit(solution)/shard_map/psum | solution.py:132
  855.4 2.6 scatter_custom_fusion.101
  867.9 19.4 %all-reduce.4 = (f32[3,1,512]{2,1,0:T(1,128)S(1)}, f32[1,512]{1,0:T(1,128)S(1)}) all-reduce(f32[3,1,512]{2,1,0:T(1,128)S(1)} %pad_maximum_fusion.15, f32[1,512]{1,0:T(1,128)S(1)} %bitcast.1047), channel_id=1, replica_groups=mesh['grp'=2,'bl'=4,'ch'=2,'pol'=2] {'bl','ch'}, use_global_device_ids=true, to_apply=%region_157.158 | all-reduce | flops 2048 | bytes 16384 | tf_op jit(solution)/shard_map/psum | solution.py:132
  900.1 2.7 scatter_custom_fusion.108
  910.1 17.4 %psum.279 = f32[3,1,512]{2,1,0:T(1,128)S(1)} all-reduce(f32[3,1,512]{2,1,0:T(1,128)S(1)} %pad_maximum_fusion.16), channel_id=1, replica_groups=mesh['grp'=2,'bl'=4,'ch'=2,'pol'=2] {'bl','ch'}, use_global_device_ids=true, to_apply=%region_167.168 | all-reduce | flops 1536 | bytes 12288 | tf_op jit(solution)/shard_map/psum | solution.py:132
  936.2 4.5 add_subtract_fusion
  940.7 4.6 subtract_subtract_fusion
  (452 shorter events, 384.5 us)
Async XLA Ops:
  0.6 39.2 %copy-start = (f32[2,512]{1,0:T(2,128)S(1)}, f32[2,512]{1,0:T(2,128)}, u32[]{:S(2)}) copy-start(f32[2,512]{1,0:T(2,128)} %param.11) | copy-start | bytes 12292
  1.6 0.7 copy-start.10
  2.3 161.1 %copy-start.49 = (s32[1,256]{1,0:T(1,128)}, s32[1,256]{1,0:T(1,128)S(1)}, u32[]{:S(2)}) copy-start(s32[1,256]{1,0:T(1,128)S(1)} %get-tuple-element.308) | copy-start | bytes 3076
  2.3 163.4 %copy-start.48 = (s32[1,256]{1,0:T(1,128)}, s32[1,256]{1,0:T(1,128)S(1)}, u32[]{:S(2)}) copy-start(s32[1,256]{1,0:T(1,128)S(1)} %get-tuple-element.307) | copy-start | bytes 3076
  2.3 0.7 copy-start.9
  23.7 0.7 copy-start.24
  38.4 58.8 %copy-start.46 = (f32[128]{0:T(128)}, f32[128]{0:T(128)S(1)}, u32[]{:S(2)}) copy-start(f32[128]{0:T(128)S(1)} %get-tuple-element.46) | copy-start | bytes 1540
  38.4 172.9 %copy-start.34 = (f32[128]{0:T(128)}, f32[128]{0:T(128)S(1)}, u32[]{:S(2)}) copy-start(f32[128]{0:T(128)S(1)} %get-tuple-element.47) | copy-start | bytes 1540
  38.4 279.1 %copy-start.32 = (f32[128]{0:T(128)}, f32[128]{0:T(128)S(1)}, u32[]{:S(2)}) copy-start(f32[128]{0:T(128)S(1)} %get-tuple-element.53) | copy-start | bytes 1540
  38.4 279.1 %copy-start.36 = (f32[128]{0:T(128)}, f32[128]{0:T(128)S(1)}, u32[]{:S(2)}) copy-start(f32[128]{0:T(128)S(1)} %get-tuple-element.48) | copy-start | bytes 1540
  38.4 387.1 %copy-start.38 = (f32[128]{0:T(128)}, f32[128]{0:T(128)S(1)}, u32[]{:S(2)}) copy-start(f32[128]{0:T(128)S(1)} %get-tuple-element.49) | copy-start | bytes 1540
  38.4 493.3 %copy-start.40 = (f32[128]{0:T(128)}, f32[128]{0:T(128)S(1)}, u32[]{:S(2)}) copy-start(f32[128]{0:T(128)S(1)} %get-tuple-element.50) | copy-start | bytes 1540
  38.4 0.7 copy-start.8
  44.9 6.4 copy-start.1
  97.1 0.6 copy-start.18
  97.1 220.4 %copy-start.16 = (f32[256]{0:T(256)}, f32[256]{0:T(256)S(1)}, u32[]{:S(2)}) copy-start(f32[256]{0:T(256)S(1)} %get-tuple-element.264) | copy-start | bytes 3076
  299.7 17.8 %copy-start.20 = (f32[256]{0:T(256)}, f32[256]{0:T(256)S(1)}, u32[]{:S(2)}) copy-start(f32[256]{0:T(256)S(1)} %get-tuple-element.228) | copy-start | bytes 3076
  299.7 17.8 %copy-start.22 = (f32[256]{0:T(256)}, f32[256]{0:T(256)S(1)}, u32[]{:S(2)}) copy-start(f32[256]{0:T(256)S(1)} %get-tuple-element.229) | copy-start | bytes 3076
  639.2 1.3 copy-start.2
  639.2 1.3 copy-start.3
  640.6 0.7 copy-start.11
  640.6 0.7 copy-start.42
  643.6 0.6 copy-start.26
  649.1 0.7 copy-start.25
  659.7 0.7 copy-start.27
  731.2 2.6 copy-start.5
  753.4 0.7 copy-start.13
  753.4 0.7 copy-start.44
  757.1 0.6 copy-start.30
  762.6 0.6 copy-start.29
  762.6 0.7 copy-start.28
  773.5 0.7 copy-start.31
  844.8 2.0 copy-start.4
  846.8 0.9 copy-start.6
  846.8 1.0 copy-start.7
  931.5 4.1 copy-start.19
  931.5 4.1 copy-start.43
  931.5 4.1 copy-start.45
  931.5 4.1 copy-start.47
  933.5 2.1 copy-start.14
  933.5 2.1 copy-start.15
  933.5 2.1 copy-start.17
  933.5 2.1 copy-start.21
  933.5 2.1 copy-start.23
  933.5 2.1 copy-start.35
  933.5 2.1 copy-start.37
  933.5 2.1 copy-start.39
  933.5 2.1 copy-start.41
  935.5 0.7 copy-start.12
  935.5 0.7 copy-start.33
  946.3 0.6 copy-start.50
where the time goes:
time: 958 us; the launch traced here: 947 us
  blocking collectives  430 us (45%)
  other arithmetic  310 us (32%)
  local copies, waits for them, and re-layouts  184 us (19%)
  between operations  23.2 us (2%)
    psum x16, blocking collectives, on_device(): totals = lax.psum(partial_value, ('bl', 'ch'))  297 us
    scatter-add x112, other arithmetic, segsum(): return jax.ops.segment_sum(values.T, index, stations).T  276 us
    all_gather x8, blocking collectives, on_device(): beam_dir = lax.all_gather(beam[direction], 'bl', axis=3, tiled=True)  119 us

commit v1 on v0

v1 whole, which is shorter than its diff:
```python
import functools
import math

import jax
import jax.numpy as jnp
import numpy as np
from jax import lax
from jax.experimental import pallas as pl
from jax.experimental.pallas import tpu as pltpu
from jax.sharding import PartitionSpec as P

NC = 256
DIRS = 8
MIXING = 0.5
VMEM_LIMIT = 48 * 1024 * 1024


def turn_polynomials():
    x = (np.cos(np.pi * (np.arange(400) + 0.5) / 400) + 1) / 8
    root = np.sqrt(x)
    fit = np.polynomial.polynomial.Polynomial.fit
    sine = fit(x, np.sin(2 * np.pi * root) / root, 7, domain=[0, 0.25], window=[0, 0.25]).coef
    cosine = fit(x, np.cos(2 * np.pi * root), 8, domain=[0, 0.25], window=[0, 0.25]).coef
    return ([float(c) for c in sine], [float(c) for c in cosine])


SINE, COSINE = turn_polynomials()


def horner(coefs, z):
    total = jnp.full_like(z, coefs[-1])
    for c in coefs[-2::-1]:
        total = total * z + c
    return total


def phasor(turns):
    rest = turns - jnp.round(turns)
    z = rest * rest
    return horner(COSINE, z), rest * horner(SINE, z)


def row_of(d):
    return 3 * d + d * (d - 1)


ROWS = row_of(DIRS)


def terms(value, count):
    parts = []
    for _ in range(count):
        part = value.astype(jnp.bfloat16)
        parts.append(part)
        value = value - part.astype(jnp.float32)
    return parts


def look_up(value, hot, count):
    m = value.shape[0]
    out = jnp.dot(
        jnp.concatenate(terms(value, count), axis=0), hot, preferred_element_type=jnp.float32
    )
    return sum(out[k * m : (k + 1) * m] for k in range(1, count)) + out[:m]


def add_up(value, hot, count):
    m = value.shape[0]
    out = lax.dot_general(
        jnp.concatenate(terms(value, count), axis=0),
        hot,
        (((1,), (1,)), ((), ())),
        preferred_element_type=jnp.float32,
    )
    return sum(out[k * m : (k + 1) * m] for k in range(1, count)) + out[:m]


def fill_hot(pairs_ref, hot):
    stations, n = hot.shape
    nb = n // 2
    ids = lax.broadcasted_iota(jnp.int32, (stations, nb), 0)
    for side in range(2):
        hot[:, side * nb : (side + 1) * nb] = jnp.where(
            ids == pairs_ref[side : side + 1, :], 1.0, 0.0
        ).astype(jnp.bfloat16)


def model_kernel(lm_ref, beam_ref, vis_ref, flux_ref, freq_ref, pos_ref, pairs_ref, model_ref, sums_ref, hot):
    nb = pairs_ref.shape[1]
    k = freq_ref.shape[0]
    fill_hot(pairs_ref, hot)
    at = look_up(pos_ref[...], hot[...], 3)
    apart = at[:, :nb] - at[:, nb:]
    live = jnp.where(pairs_ref[0:1, :] != pairs_ref[1:2, :], 1.0, 0.0)
    freq = freq_ref[...]

    def row(value):
        return jnp.sum(value, axis=0, keepdims=True)

    for d in range(DIRS):
        turns = freq * (apart[0:1] * lm_ref[d, 0] + apart[1:2] * lm_ref[d, 1])
        cosine, sine = phasor(turns)
        e_r, e_i = beam_ref[d, 0], beam_ref[d, 1]
        both_r = look_up(e_r, hot[...], 2)
        both_i = look_up(e_i, hot[...], 2)
        left_r, right_r = both_r[:, :nb], both_r[:, nb:]
        left_i, right_i = both_i[:, :nb], both_i[:, nb:]
        cross_r = left_r * right_r + left_i * right_i
        cross_i = left_i * right_r - left_r * right_i
        scale = flux_ref[d] * live
        m_r = (cross_r * cosine - cross_i * sine) * scale
        m_i = (cross_r * sine + cross_i * cosine) * scale
        model_ref[d, 0] = m_r
        model_ref[d, 1] = m_i
        v_r, v_i = vis_ref[0], vis_ref[1]
        at_row = row_of(d)
        sums_ref[at_row : at_row + 1] = row(m_r * m_r + m_i * m_i)
        sums_ref[at_row + 1 : at_row + 2] = row(v_r * m_r + v_i * m_i)
        sums_ref[at_row + 2 : at_row + 3] = row(v_i * m_r - v_r * m_i)
        for e in range(d):
            o_r, o_i = model_ref[e, 0], model_ref[e, 1]
            b = at_row + 3 + 2 * e
            sums_ref[b : b + 1] = row(o_r * m_r + o_i * m_i)
            sums_ref[b + 1 : b + 2] = row(o_i * m_r - o_r * m_i)


def solve_kernel(pairs_ref, sums_ref, vis_ref, model_ref, res_ref, gains_ref, hot, pair):
    nb = pairs_ref.shape[1]
    fill_hot(pairs_ref, hot)
    power = jnp.concatenate([sums_ref[row_of(d) : row_of(d) + 1] for d in range(DIRS)], axis=0)
    weights = add_up(jnp.concatenate([power, power], axis=1), hot[...], 3)

    for d in range(DIRS):
        at_row = row_of(d)
        q = sums_ref[at_row : at_row + 1]
        p_r = sums_ref[at_row + 1 : at_row + 2]
        p_i = sums_ref[at_row + 2 : at_row + 3]
        for e in range(d):
            b = at_row + 3 + 2 * e
            b_r, b_i = sums_ref[b : b + 1], sums_ref[b + 1 : b + 2]
            g_r, g_i = pair[2 * e : 2 * e + 1], pair[2 * e + 1 : 2 * e + 2]
            p_r = p_r - (g_r * b_r - g_i * b_i)
            p_i = p_i - (g_r * b_i + g_i * b_r)
        w = weights[d : d + 1]
        first = add_up(
            jnp.concatenate(
                [jnp.concatenate([p_r, p_r], axis=1), jnp.concatenate([p_i, -p_i], axis=1)], axis=0
            ),
            hot[...],
            3,
        )
        scale = 0.5 / (w + MIXING * w + 1.0)
        gain_r = 0.5 + (first[0:1] + MIXING * w + 1.0) * scale
        gain_i = first[1:2] * scale
        at = look_up(jnp.concatenate([gain_r, gain_i], axis=0), hot[...], 3)
        near_r, far_r = at[0:1, :nb], at[0:1, nb:]
        near_i, far_i = at[1:2, :nb], at[1:2, nb:]
        head = [p_r * far_r - p_i * far_i, p_r * far_i + p_i * far_r, q * (far_r * far_r + far_i * far_i)]
        tail = [p_r * near_r + p_i * near_i, p_r * near_i - p_i * near_r, q * (near_r * near_r + near_i * near_i)]
        second = add_up(
            jnp.concatenate([jnp.concatenate([h, t], axis=1) for h, t in zip(head, tail)], axis=0),
            hot[...],
            3,
        )
        scale = 0.5 / (second[2:3] + MIXING * w + 1.0)
        gain_r = 0.5 * gain_r + (second[0:1] + MIXING * w + 1.0) * scale
        gain_i = 0.5 * gain_i + second[1:2] * scale
        gains = jnp.concatenate([gain_r, gain_i], axis=0)
        gains_ref[d] = gains
        at = look_up(gains, hot[...], 3)
        near_r, far_r = at[0:1, :nb], at[0:1, nb:]
        near_i, far_i = at[1:2, :nb], at[1:2, nb:]
        pair[2 * d : 2 * d + 1] = near_r * far_r + near_i * far_i
        pair[2 * d + 1 : 2 * d + 2] = near_i * far_r - near_r * far_i

    r_r, r_i = vis_ref[0], vis_ref[1]
    for d in range(DIRS):
        g_r, g_i = pair[2 * d : 2 * d + 1], pair[2 * d + 1 : 2 * d + 2]
        m_r, m_i = model_ref[d, 0], model_ref[d, 1]
        r_r = r_r - (g_r * m_r - g_i * m_i)
        r_i = r_i - (g_r * m_i + g_i * m_r)
    res_ref[0] = r_r
    res_ref[1] = r_i


def on_device(n_bl, visibilities, beam, coherency, owner, positions, direction_lm, pairs):
    chans = visibilities.shape[2]
    k = chans // n_bl
    stations = positions.shape[1]
    nb = pairs.shape[1] * n_bl
    start = lax.axis_index("ch") * chans + lax.axis_index("bl") * k
    freq = 1.0 + 0.5 * (start + jnp.arange(k)).astype(jnp.float32)[:, None] / NC
    all_pairs = lax.all_gather(pairs, "bl", axis=1, tiled=True)
    e = lax.all_to_all(beam[:, :, 0], "bl", split_axis=2, concat_axis=3, tiled=True)
    v = lax.all_to_all(visibilities[:, 0], "bl", split_axis=1, concat_axis=2, tiled=True)
    table = lax.all_to_all(coherency[:, 0], "bl", split_axis=1, concat_axis=0, tiled=True)
    flux = table[owner][:, :, None]
    vmem = pl.BlockSpec(memory_space=pltpu.VMEM)
    model, sums = pl.pallas_call(
        model_kernel,
        out_shape=(
            jax.ShapeDtypeStruct((DIRS, 2, k, nb), jnp.float32),
            jax.ShapeDtypeStruct((ROWS, nb), jnp.float32),
        ),
        in_specs=[pl.BlockSpec(memory_space=pltpu.SMEM)] + [vmem] * 6,
        out_specs=(vmem, vmem),
        scratch_shapes=[pltpu.VMEM((stations, 2 * nb), jnp.bfloat16)],
        compiler_params=pltpu.CompilerParams(vmem_limit_bytes=VMEM_LIMIT),
        name="model",
    )(direction_lm, e, v, flux, freq, positions, all_pairs)
    sums = lax.psum(sums, ("bl", "ch"))
    res, gains = pl.pallas_call(
        solve_kernel,
        out_shape=(
            jax.ShapeDtypeStruct((2, k, nb), jnp.float32),
            jax.ShapeDtypeStruct((DIRS, 2, stations), jnp.float32),
        ),
        in_specs=[vmem] * 4,
        out_specs=(vmem, vmem),
        scratch_shapes=[
            pltpu.VMEM((stations, 2 * nb), jnp.bfloat16),
            pltpu.VMEM((2 * DIRS, nb), jnp.float32),
        ],
        compiler_params=pltpu.CompilerParams(vmem_limit_bytes=VMEM_LIMIT),
        name="solve",
    )(all_pairs, sums, v, model)
    res = lax.all_to_all(res, "bl", split_axis=2, concat_axis=1, tiled=True)
    return (res[:, None], gains[:, :, None])


def solution(mesh):
    return jax.shard_map(
        functools.partial(on_device, mesh.shape["bl"]),
        mesh=mesh,
        in_specs=(
            P(None, "pol", "ch", ("grp", "bl")),
            P("grp", None, "pol", "ch", "bl"),
            P(("grp", "bl"), "pol", "ch"),
            P("grp"),
            P(None, "grp"),
            P("grp", None),
            P(None, ("grp", "bl")),
        ),
        out_specs=(P(None, "pol", "ch", ("grp", "bl")), P("grp", None, "pol", None)),
        check_vma=False,
    )
```

time: 958 us -> 190 us (0.20); the launches traced: 947 us -> 189 us
  blocking collectives: 430 us -> 28.7 us
  other arithmetic: 310 us -> 3.34 us
  local copies, waits for them, and re-layouts: 184 us -> 16.2 us
  waiting for transfers between devices: 0 us -> 84.1 us
  Pallas kernels: 0 us -> 25.9 us
  starting transfers between devices: 0 us -> 16.9 us
    psum x17 -> x0, blocking collectives: 311 us -> none  [the longest x16 297 us: on_device(): totals = lax.psum(partial_value, ('bl', 'ch'))]
    scatter-add x112 -> x0, other arithmetic: 276 us -> none  [segsum(): return jax.ops.segment_sum(values.T, index, stations).T]
    gather x104 -> x1, local copies, waits for them, and re-layouts: 169 us -> 0.55 us  [on_device(): flux = table[owner][:, :, None]]
    all_gather x8 -> x1, blocking collectives: 119 us -> 28.7 us  [on_device(): all_pairs = lax.all_gather(pairs, 'bl', axis=1, tiled=True)]
    psum x0 -> x1, waiting for transfers between devices: none -> 69.4 us  [on_device(): sums = lax.psum(sums, ('bl', 'ch'))]
    pallas_call x0 -> x2, Pallas kernels: none -> 25.9 us  [the longest x1 17.2 us: on_device(): pl.pallas_call(solve_kernel, out_shape=(jax.ShapeDtypeStruct((2, k, nb),...]
    all_to_all x0 -> x4, starting transfers between devices: none -> 16.9 us  [the longest x1 6.32 us: on_device(): lax.all_to_all(coherency[:, 0], 'bl', split_axis=1, concat_axis=0, tiled=...]
    all_to_all x0 -> x4, waiting for transfers between devices: none -> 14.7 us  [the longest x1 6.13 us: on_device(): res = lax.all_to_all(res, 'bl', split_axis=2, concat_axis=1, tiled=True)]
  transfers between devices with their start and end apart: 0 -> 5, of which waited for: 0 -> 4; matrix products, arithmetic and copies ran while one was open for 0% -> 4% of each run, Pallas kernels for 0% -> 0%
where the time goes in v1:
time: 190 us; the launch traced here: 189 us
  waiting for transfers between devices  84.1 us (44%)
  blocking collectives  28.7 us (15%)
  Pallas kernels  25.9 us (14%)
  starting transfers between devices  16.9 us (9%)
  local copies, waits for them, and re-layouts  16.2 us (9%)
  between operations  14.2 us (7%)
  other arithmetic  3.34 us (2%)
    psum x1, waiting for transfers between devices, on_device(): sums = lax.psum(sums, ('bl', 'ch'))  69.4 us
    all_gather x1, blocking collectives, on_device(): all_pairs = lax.all_gather(pairs, 'bl', axis=1, tiled=True)  28.7 us
    pallas_call x1, Pallas kernels, on_device(): pl.pallas_call(solve_kernel, out_shape=(jax.ShapeDtypeStruct((2, k, nb),...  17.2 us
    unnamed x21, local copies, waits for them, and re-layouts  11.2 us
    pallas_call x1, Pallas kernels, on_device(): pl.pallas_call(model_kernel, out_shape=(jax.ShapeDtypeStruct((DIRS, 2, k,...  8.76 us
    all_to_all x1, starting transfers between devices, on_device(): lax.all_to_all(coherency[:, 0], 'bl', split_axis=1, concat_axis=0, tiled=...  6.32 us
    all_to_all x1, waiting for transfers between devices, on_device(): res = lax.all_to_all(res, 'bl', split_axis=2, concat_axis=1, tiled=True)  6.13 us
    all_to_all x1, waiting for transfers between devices, on_device(): lax.all_to_all(visibilities[:, 0], 'bl', split_axis=1, concat_axis=2, til...  4.83 us
  transfers between devices with their start and end apart: 5, of which 4 were waited for; matrix products, arithmetic and copies ran while one was open for 4% of the time, Pallas kernels for 0%

profile of v1, /device:TPU:0, one launch (start us, length us, event | category | flops | bytes accessed | tf_op | source)
XLA Modules:
  0.0 189.2 jit_solution(1552223217695698858)
XLA Ops:
  7.2 0.5 broadcast.44
  7.7 1.3 reduce.3
  9.0 0.1 all_to_all.59
  9.1 0.6 copy.36
  9.7 6.3 %all-to-all-start.2 = ((f32[2,4,32]{2,0,1:T(2,128)}), f32[2,4,32]{2,0,1:T(2,128)S(1)}, u32[]{:S(2)}, u32[]{:S(2)}) async-start(f32[2,4,32]{2,0,1:T(2,128)} %copy.36), calls=%async_computation.2 | async-start | bytes 8192 | tf_op jit(solution)/shard_map/all_to_all | solution.py:196
  16.0 1.9 copy.50
  17.9 3.7 %all-to-all-done.2 = f32[2,4,32]{2,0,1:T(2,128)S(1)} async-done(((f32[2,4,32]{2,0,1:T(2,128)}), f32[2,4,32]{2,0,1:T(2,128)S(1)}, u32[]{:S(2)}, u32[]{:S(2)}) %all-to-all-start.2) | async-done | bytes 1056 | tf_op jit(solution)/shard_map/all_to_all | solution.py:196
  21.6 3.4 %all-to-all-start.1 = ((f32[2,128,256]{2,0,1:T(2,128)}), f32[2,128,256]{2,0,1:T(2,128)S(1)}, u32[]{:S(2)}, u32[]{:S(2)}) async-start(f32[2,128,256]{2,0,1:T(2,128)} %bitcast.24), calls=%async_computation.1 | async-start | bytes 524288 | tf_op jit(solution)/shard_map/all_to_all | solution.py:195
  25.0 0.0 copy-start.5
  25.0 0.0 copy-start.4
  25.0 0.0 copy-start.6
  25.0 3.0 %copy.48 = f32[8,2,1,128,128]{4,1,0,3,2:T(2,128)} copy(f32[8,2,1,128,128]{4,3,2,1,0:T(8,128)} %param.8) | data formatting | bytes 2097152 | tf_op args[1]
  28.1 4.8 %all-to-all-done.1 = f32[2,128,256]{2,0,1:T(2,128)S(1)} async-done(((f32[2,128,256]{2,0,1:T(2,128)}), f32[2,128,256]{2,0,1:T(2,128)S(1)}, u32[]{:S(2)}, u32[]{:S(2)}) %all-to-all-start.1) | async-done | bytes 262176 | tf_op jit(solution)/shard_map/all_to_all | solution.py:195
  32.9 3.5 %all-to-all-start = ((f32[8,2,128,128]{3,1,0,2:T(2,128)}), f32[8,2,128,128]{3,1,0,2:T(2,128)S(1)}, u32[]{:S(2)}, u32[]{:S(2)}) async-start(f32[8,2,128,128]{3,1,0,2:T(2,128)} %bitcast.22), calls=%async_computation | async-start | bytes 2097152 | tf_op jit(solution)/shard_map/all_to_all | solution.py:194
  36.4 0.0 all-reduce.2.cloned.1.call-start
  36.5 0.0 copy-done.5
  36.5 0.1 copy.38.lm_ref
  36.6 0.0 copy-done.4
  36.6 28.7 %all_gather.3.pairs_ref = s32[2,1024]{1,0:T(2,128)S(1)} all-gather(s32[2,256]{1,0:T(2,128)S(1)} %copy-done.4), channel_id=1, replica_groups=mesh['grp'=2,'bl'=4,'ch'=2,'pol'=2] {'bl'}, dimensions={1}, use_global_device_ids=true | all-gather | bytes 10240 | tf_op jit(solution)/shard_map/all_gather | solution.py:193
  65.2 0.0 copy-done.6
  65.3 0.6 multiply_add_fusion.freq_ref
  65.9 0.6 gather_fusion
  66.4 0.1 copy.39.flux_ref
  66.6 0.2 copy.49
  66.7 0.1 all_to_all.58.vis_ref
  66.9 0.0 all-to-all-done
  66.9 0.0 copy-start.3
  66.9 0.7 copy.47
  67.6 0.4 all_to_all.54.beam_ref
  68.0 0.0 copy-done.3
  68.0 0.0 copy-start.2
  68.0 0.7 copy-done.2
  68.8 8.8 %model.1 = (f32[8,2,32,1024]{3,2,1,0:T(8,128)S(1)}, f32[80,1024]{1,0:T(8,128)S(1)}) custom-call(f32[8,2]{1,0:T(8,128)S(1)} %copy.38.lm_ref, f32[8,2,32,512]{3,2,1,0:T(8,128)S(1)} %all_to_all.54.beam_ref, f32[2,32,1024]{2,1,0:T(8,128)S(1)} %all_to_all.58.vis_ref, f32[8,32,1]{2,1,0:T(8,128)S(1)} %copy.39.flux_ref, f32[32,1]{1,0:T(8,128)S(1)} %copy-done.2, ...), custom_call_target="tpu_custom_call" | custom-call | tf_op jit(solution)/shard_map/model/pallas_call | solution.py:199
  77.5 0.0 copy-start
  77.5 0.7 copy-done
  78.2 0.0 all-reduce.2.cloned.1.call-update
  78.3 69.4 %all-reduce.2.cloned.1.call-done.sums_ref = f32[80,1024]{1,0:T(8,128)} async-done(((f32[80,1024]{1,0:T(8,128)}), f32[80,1024]{1,0:T(8,128)}) %all-reduce.2.cloned.1.call-update) | async-done | bytes 327696 | tf_op jit(solution)/shard_map/psum | solution.py:211
  147.6 0.0 copy-start.1
  147.6 1.0 copy-done.1
  148.6 17.2 %solve.1 = (f32[2,32,1024]{2,1,0:T(8,128)S(1)}, f32[8,2,512]{2,1,0:T(2,128)S(1)}) custom-call(s32[2,1024]{1,0:T(2,128)S(1)} %all_gather.3.pairs_ref, f32[80,1024]{1,0:T(8,128)S(1)} %copy-done.1, f32[2,32,1024]{2,1,0:T(8,128)S(1)} %all_to_all.58.vis_ref, f32[8,2,32,1024]{3,2,1,0:T(8,128)S(1)} %get-tuple-element.7.model_ref), custom_call_target="tpu_custom_call" | custom-call | tf_op jit(solution)/shard_map/solve/pallas_call | solution.py:212
  165.8 0.5 copy.40
  166.3 1.8 reshape.46
  168.1 3.6 %all-to-all-start.3 = ((f32[4,1,16384]{2,1,0:T(1,128)}), f32[4,1,16384]{2,1,0:T(1,128)S(1)}, u32[]{:S(2)}, u32[]{:S(2)}) async-start(f32[4,1,16384]{2,1,0:T(1,128)} %reshape.46), calls=%async_computation.3 | async-start | bytes 524288 | tf_op jit(solution)/shard_map/all_to_all | solution.py:227
  171.7 0.6 copy.42
  172.3 6.1 %all-to-all-done.3 = f32[4,1,16384]{2,1,0:T(1,128)S(1)} async-done(((f32[4,1,16384]{2,1,0:T(1,128)}), f32[4,1,16384]{2,1,0:T(1,128)S(1)}, u32[]{:S(2)}, u32[]{:S(2)}) %all-to-all-start.3) | async-done | bytes 262176 | tf_op jit(solution)/shard_map/all_to_all | solution.py:227
  178.5 0.5 broadcast.45
  179.0 1.4 reduce.4
  180.4 0.9 reshape.47
  181.3 1.1 copy.41
  (2 shorter events, 0.0 us)
Async XLA Ops:
  9.7 11.9 %all-to-all-start.2 = ((f32[2,4,32]{2,0,1:T(2,128)}), f32[2,4,32]{2,0,1:T(2,128)S(1)}, u32[]{:S(2)}, u32[]{:S(2)}) async-start(f32[2,4,32]{2,0,1:T(2,128)} %copy.36), calls=%async_computation.2 | async-start | bytes 8192 | tf_op jit(solution)/shard_map/all_to_all | solution.py:196
  21.6 11.3 %all-to-all-start.1 = ((f32[2,128,256]{2,0,1:T(2,128)}), f32[2,128,256]{2,0,1:T(2,128)S(1)}, u32[]{:S(2)}, u32[]{:S(2)}) async-start(f32[2,128,256]{2,0,1:T(2,128)} %bitcast.24), calls=%async_computation.1 | async-start | bytes 524288 | tf_op jit(solution)/shard_map/all_to_all | solution.py:195
  25.0 11.5 %copy-start.5 = (f32[8,2]{0,1:T(2,128)S(1)}, f32[8,2]{0,1:T(2,128)}, u32[]{:S(2)}) copy-start(f32[8,2]{0,1:T(2,128)} %param.12) | copy-start | bytes 196
  25.0 11.5 %copy-start.4 = (s32[2,256]{1,0:T(2,128)S(1)}, s32[2,256]{1,0:T(2,128)}, u32[]{:S(2)}) copy-start(s32[2,256]{1,0:T(2,128)} %param.13) | copy-start | bytes 6148
  25.0 40.2 %copy-start.6 = (s32[8]{0:T(128)S(1)}, s32[8]{0:T(128)}, u32[]{:S(2)}) copy-start(s32[8]{0:T(128)} %param.10) | copy-start | bytes 100
  32.9 34.0 %all-to-all-start = ((f32[8,2,128,128]{3,1,0,2:T(2,128)}), f32[8,2,128,128]{3,1,0,2:T(2,128)S(1)}, u32[]{:S(2)}, u32[]{:S(2)}) async-start(f32[8,2,128,128]{3,1,0,2:T(2,128)} %bitcast.22), calls=%async_computation | async-start | bytes 2097152 | tf_op jit(solution)/shard_map/all_to_all | solution.py:194
  36.4 111.2 %all-reduce.2.cloned.1.call-start = ((), (), s32[]{:S(2)}) async-start(), calls=%async_computation.4 | async-start | bytes 655360 | tf_op jit(solution)/shard_map/psum | solution.py:211
  66.9 1.1 copy-start.3
  68.0 0.7 copy-start.2
  77.5 0.7 copy-start
  147.6 1.0 copy-start.1
  168.1 10.4 %all-to-all-start.3 = ((f32[4,1,16384]{2,1,0:T(1,128)}), f32[4,1,16384]{2,1,0:T(1,128)S(1)}, u32[]{:S(2)}, u32[]{:S(2)}) async-start(f32[4,1,16384]{2,1,0:T(1,128)} %reshape.46), calls=%async_computation.3 | async-start | bytes 524288 | tf_op jit(solution)/shard_map/all_to_all | solution.py:227
Sparse Core Ops, SparseCore 0:
  78.4 69.1 all-reduce.1

commit v2 on v1

v2 whole, which is shorter than its diff:
```python
import functools
import math

import jax
import jax.numpy as jnp
import numpy as np
from jax import lax
from jax.experimental import pallas as pl
from jax.experimental.pallas import tpu as pltpu
from jax.sharding import PartitionSpec as P

NC = 256
DIRS = 8
MIXING = 0.5
VMEM_LIMIT = 48 * 1024 * 1024


def turn_polynomials():
    x = (np.cos(np.pi * (np.arange(400) + 0.5) / 400) + 1) / 8
    root = np.sqrt(x)
    fit = np.polynomial.polynomial.Polynomial.fit
    sine = fit(x, np.sin(2 * np.pi * root) / root, 7, domain=[0, 0.25], window=[0, 0.25]).coef
    cosine = fit(x, np.cos(2 * np.pi * root), 8, domain=[0, 0.25], window=[0, 0.25]).coef
    return ([float(c) for c in sine], [float(c) for c in cosine])


SINE, COSINE = turn_polynomials()


def horner(coefs, z):
    total = jnp.full_like(z, coefs[-1])
    for c in coefs[-2::-1]:
        total = total * z + c
    return total


def phasor(turns):
    rest = turns - jnp.round(turns)
    z = rest * rest
    return horner(COSINE, z), rest * horner(SINE, z)


def row_of(d):
    return 3 * d + d * (d - 1)


ROWS = row_of(DIRS)


def terms(value, count):
    parts = []
    for _ in range(count):
        part = value.astype(jnp.bfloat16)
        parts.append(part)
        value = value - part.astype(jnp.float32)
    return parts


def look_up(value, hot, count):
    m = value.shape[0]
    out = jnp.dot(
        jnp.concatenate(terms(value, count), axis=0), hot, preferred_element_type=jnp.float32
    )
    return sum(out[k * m : (k + 1) * m] for k in range(1, count)) + out[:m]


def add_up(value, hot, count):
    m = value.shape[0]
    out = lax.dot_general(
        jnp.concatenate(terms(value, count), axis=0),
        hot,
        (((1,), (1,)), ((), ())),
        preferred_element_type=jnp.float32,
    )
    return sum(out[k * m : (k + 1) * m] for k in range(1, count)) + out[:m]


def one_kernel(
    n_bl, n_ch,
    lm_ref, owner_ref, freq_ref, pos_ref, pairs_ref, coh_ref, vis_ref, beam_ref,
    res_ref, gains_ref,
    pairs_in, coh_in, vis_in, beam_in, hot, model, part, part_in, total, full, pair, res_out, res_in,
    ex_send, ex_recv, sum_send, sum_recv, all_send, all_recv, back_send, back_recv,
):
    k = freq_ref.shape[0]
    nb_loc = pairs_ref.shape[1]
    nb = nb_loc * n_bl
    n = n_bl * n_ch
    rp = total.shape[0]
    stations = pos_ref.shape[1]
    slot_dev = coh_ref.shape[1]
    my_bl, my_ch = lax.axis_index("bl"), lax.axis_index("ch")
    me = my_bl * n_ch + my_ch

    def peer(off):
        return lax.rem(me + off, n)

    def place(p):
        return {"bl": lax.div(p, n_ch), "ch": lax.rem(p, n_ch)}

    barrier = pltpu.get_barrier_semaphore()

    def greet(off, _):
        pl.semaphore_signal(barrier, inc=1, device_id=place(peer(off)), device_id_type=pl.DeviceIdType.MESH)
        return 0

    lax.fori_loop(1, n, greet, 0)
    pl.semaphore_wait(barrier, n - 1)

    def source(kind, to):
        if kind == 0:
            return pairs_ref
        if kind == 1:
            return coh_ref.at[to]
        if kind == 2:
            return vis_ref.at[:, to]
        return beam_ref.at[kind - 3, :, to]

    def landing(kind, frm):
        if kind == 0:
            return pairs_in.at[frm]
        if kind == 1:
            return coh_in.at[frm]
        if kind == 2:
            return vis_in.at[frm]
        return beam_in.at[kind - 3, frm]

    def own(kind):
        return pltpu.make_async_copy(source(kind, my_bl), landing(kind, my_bl), ex_recv.at[kind, my_bl])

    def exchange(kind, to, frm):
        return pltpu.make_async_remote_copy(
            src_ref=source(kind, to),
            dst_ref=landing(kind, frm),
            send_sem=ex_send.at[kind, to],
            recv_sem=ex_recv.at[kind, frm],
            device_id={"bl": to},
            device_id_type=pl.DeviceIdType.MESH,
        )

    kinds = 3 + DIRS
    for kind in range(kinds):
        for off in range(1, n_bl):
            exchange(kind, lax.rem(my_bl + off, n_bl), my_bl).start()
        own(kind).start()

    def arrived(kind):
        own(kind).wait()
        for off in range(1, n_bl):
            frm = lax.rem(my_bl + n_bl - off, n_bl)
            exchange(kind, frm, frm).wait_recv()

    arrived(0)
    ids = lax.broadcasted_iota(jnp.int32, (stations, nb_loc), 0)
    live_parts = []
    for frm in range(n_bl):
        for side in range(2):
            at = side * nb + frm * nb_loc
            hot[:, at : at + nb_loc] = jnp.where(
                ids == pairs_in[frm, side : side + 1, :], 1.0, 0.0
            ).astype(jnp.bfloat16)
        live_parts.append(
            jnp.where(pairs_in[frm, 0:1, :] != pairs_in[frm, 1:2, :], 1.0, 0.0)
        )
    live = jnp.concatenate(live_parts, axis=1)
    at = look_up(pos_ref[...], hot[...], 3)
    apart = at[:, :nb] - at[:, nb:]
    freq = freq_ref[...]
    eye = lax.broadcasted_iota(jnp.int32, (k, k), 0) == lax.broadcasted_iota(jnp.int32, (k, k), 1)

    def put_row(r, value):
        line = jnp.sum(value, axis=0, keepdims=True)
        c, i = r // rp, r % rp
        for j in range(n_bl):
            part[j, c, i : i + 1, :] = line[:, j * nb_loc : (j + 1) * nb_loc]

    def get_row(r):
        c, i = r // rp, r % rp
        return jnp.concatenate([full[j, c, i : i + 1, :] for j in range(n_bl)], axis=1)

    if n_ch * rp > ROWS:
        part[...] = jnp.zeros_like(part)
    arrived(1)
    arrived(2)
    vis = [jnp.concatenate([vis_in[frm, c] for frm in range(n_bl)], axis=1) for c in range(2)]
    for d in range(DIRS):
        turns = freq * (apart[0:1] * lm_ref[d, 0] + apart[1:2] * lm_ref[d, 1])
        cosine, sine = phasor(turns)
        line = jnp.zeros((1, k), jnp.float32)
        for r in range(n_bl * slot_dev):
            line = line + jnp.where(
                owner_ref[d] == r, coh_in[r // slot_dev, r % slot_dev : r % slot_dev + 1, :], 0.0
            )
        flux = jnp.sum(jnp.where(eye, line, 0.0), axis=1, keepdims=True)
        scale = flux * live
        arrived(3 + d)
        e = jnp.concatenate(
            [
                jnp.concatenate([beam_in[d, frm, c] for frm in range(n_bl)], axis=1)
                for c in range(2)
            ],
            axis=0,
        )
        both = look_up(e, hot[...], 2)
        left_r, right_r = both[:k, :nb], both[:k, nb:]
        left_i, right_i = both[k:, :nb], both[k:, nb:]
        cross_r = left_r * right_r + left_i * right_i
        cross_i = left_i * right_r - left_r * right_i
        m_r = (cross_r * cosine - cross_i * sine) * scale
        m_i = (cross_r * sine + cross_i * cosine) * scale
        model[d, 0] = m_r
        model[d, 1] = m_i
        at_row = row_of(d)
        put_row(at_row, m_r * m_r + m_i * m_i)
        put_row(at_row + 1, vis[0] * m_r + vis[1] * m_i)
        put_row(at_row + 2, vis[1] * m_r - vis[0] * m_i)
        for f in range(d):
            o_r, o_i = model[f, 0], model[f, 1]
            put_row(at_row + 3 + 2 * f, o_r * m_r + o_i * m_i)
            put_row(at_row + 4 + 2 * f, o_i * m_r - o_r * m_i)

    def share(p, slot):
        return pltpu.make_async_remote_copy(
            src_ref=part.at[lax.div(p, n_ch), lax.rem(p, n_ch)],
            dst_ref=part_in.at[slot],
            send_sem=sum_send.at[p],
            recv_sem=sum_recv.at[slot],
            device_id=place(p),
            device_id_type=pl.DeviceIdType.MESH,
        )

    def spread(p, slot):
        return pltpu.make_async_remote_copy(
            src_ref=total,
            dst_ref=full.at[lax.div(slot, n_ch), lax.rem(slot, n_ch)],
            send_sem=all_send.at[p],
            recv_sem=all_recv.at[slot],
            device_id=place(p),
            device_id_type=pl.DeviceIdType.MESH,
        )

    def each(body):
        def step(off, _):
            body(peer(off))
            return 0

        lax.fori_loop(1, n, step, 0)

    each(lambda p: share(p, me).start())
    part_in[me] = part[my_bl, my_ch]
    each(lambda p: share(p, p).wait_recv())
    total[...] = lax.fori_loop(1, n, lambda s, acc: acc + part_in[s], part_in[0])
    each(lambda p: spread(p, me).start())
    full[my_bl, my_ch] = total[...]
    each(lambda p: spread(p, p).wait_recv())

    power = jnp.concatenate([get_row(row_of(d)) for d in range(DIRS)], axis=0)
    weights = add_up(jnp.concatenate([power, power], axis=1), hot[...], 3)
    for d in range(DIRS):
        at_row = row_of(d)
        q, p_r, p_i = get_row(at_row), get_row(at_row + 1), get_row(at_row + 2)
        for f in range(d):
            b_r, b_i = get_row(at_row + 3 + 2 * f), get_row(at_row + 4 + 2 * f)
            g_r, g_i = pair[2 * f : 2 * f + 1], pair[2 * f + 1 : 2 * f + 2]
            p_r = p_r - (g_r * b_r - g_i * b_i)
            p_i = p_i - (g_r * b_i + g_i * b_r)
        w = weights[d : d + 1]
        first = add_up(
            jnp.concatenate(
                [jnp.concatenate([p_r, p_r], axis=1), jnp.concatenate([p_i, -p_i], axis=1)], axis=0
            ),
            hot[...],
            3,
        )
        scale = 0.5 / (w + MIXING * w + 1.0)
        gain_r = 0.5 + (first[0:1] + MIXING * w + 1.0) * scale
        gain_i = first[1:2] * scale
        at = look_up(jnp.concatenate([gain_r, gain_i], axis=0), hot[...], 3)
        near_r, far_r = at[0:1, :nb], at[0:1, nb:]
        near_i, far_i = at[1:2, :nb], at[1:2, nb:]
        head = [p_r * far_r - p_i * far_i, p_r * far_i + p_i * far_r, q * (far_r * far_r + far_i * far_i)]
        tail = [p_r * near_r + p_i * near_i, p_r * near_i - p_i * near_r, q * (near_r * near_r + near_i * near_i)]
        second = add_up(
            jnp.concatenate([jnp.concatenate([h, t], axis=1) for h, t in zip(head, tail)], axis=0),
            hot[...],
            3,
        )
        scale = 0.5 / (second[2:3] + MIXING * w + 1.0)
        gain_r = 0.5 * gain_r + (second[0:1] + MIXING * w + 1.0) * scale
        gain_i = 0.5 * gain_i + second[1:2] * scale
        gains = jnp.concatenate([gain_r, gain_i], axis=0)
        gains_ref[d] = gains
        at = look_up(gains, hot[...], 3)
        near_r, far_r = at[0:1, :nb], at[0:1, nb:]
        near_i, far_i = at[1:2, :nb], at[1:2, nb:]
        pair[2 * d : 2 * d + 1] = near_r * far_r + near_i * far_i
        pair[2 * d + 1 : 2 * d + 2] = near_i * far_r - near_r * far_i

    for j in range(n_bl):
        lo, hi = j * nb_loc, (j + 1) * nb_loc
        r_r, r_i = vis_in[j, 0], vis_in[j, 1]
        for d in range(DIRS):
            g_r, g_i = pair[2 * d : 2 * d + 1, lo:hi], pair[2 * d + 1 : 2 * d + 2, lo:hi]
            m_r, m_i = model[d, 0, :, lo:hi], model[d, 1, :, lo:hi]
            r_r = r_r - (g_r * m_r - g_i * m_i)
            r_i = r_i - (g_r * m_i + g_i * m_r)
        res_out[j, 0] = r_r
        res_out[j, 1] = r_i

    def back(to, slot):
        return pltpu.make_async_remote_copy(
            src_ref=res_out.at[to],
            dst_ref=res_in.at[slot],
            send_sem=back_send.at[to],
            recv_sem=back_recv.at[slot],
            device_id={"bl": to},
            device_id_type=pl.DeviceIdType.MESH,
        )

    for off in range(1, n_bl):
        back(lax.rem(my_bl + off, n_bl), my_bl).start()
    res_in[my_bl] = res_out[my_bl]
    for off in range(1, n_bl):
        frm = lax.rem(my_bl + n_bl - off, n_bl)
        back(frm, frm).wait_recv()
    for j in range(n_bl):
        for c in range(2):
            res_ref[c, j] = res_in[j, c]

    for kind in range(kinds):
        for off in range(1, n_bl):
            to = lax.rem(my_bl + off, n_bl)
            exchange(kind, to, to).wait_send()
    each(lambda p: share(p, p).wait_send())
    each(lambda p: spread(p, p).wait_send())
    for off in range(1, n_bl):
        to = lax.rem(my_bl + off, n_bl)
        back(to, to).wait_send()


def on_device(n_bl, n_ch, visibilities, beam, coherency, owner, positions, direction_lm, pairs):
    chans = visibilities.shape[2]
    k = chans // n_bl
    stations = positions.shape[1]
    st_loc = beam.shape[4]
    nb_loc = pairs.shape[1]
    nb = nb_loc * n_bl
    slot_dev = coherency.shape[0]
    n = n_bl * n_ch
    rp = -(-ROWS // n_ch)
    start = lax.axis_index("ch") * chans + lax.axis_index("bl") * k
    freq = 1.0 + 0.5 * (start + jnp.arange(k)).astype(jnp.float32)[:, None] / NC
    coh = coherency[:, 0].reshape(slot_dev, n_bl, k).transpose(1, 0, 2)
    vis = visibilities.reshape(2, n_bl, k, nb_loc)
    beams = beam.reshape(DIRS, 2, n_bl, k, st_loc)
    vmem = pl.BlockSpec(memory_space=pltpu.VMEM)
    smem = pl.BlockSpec(memory_space=pltpu.SMEM)
    anywhere = pl.BlockSpec(memory_space=pl.ANY)
    f32 = jnp.float32
    dma = pltpu.SemaphoreType.DMA
    res, gains = pl.pallas_call(
        functools.partial(one_kernel, n_bl, n_ch),
        out_shape=(
            jax.ShapeDtypeStruct((2, n_bl, k, nb_loc), f32),
            jax.ShapeDtypeStruct((DIRS, 2, stations), f32),
        ),
        in_specs=[smem, smem, vmem, vmem, vmem, vmem, anywhere, anywhere],
        out_specs=(vmem, vmem),
        scratch_shapes=[
            pltpu.VMEM((n_bl, 2, nb_loc), jnp.int32),
            pltpu.VMEM((n_bl, slot_dev, k), f32),
            pltpu.VMEM((n_bl, 2, k, nb_loc), f32),
            pltpu.VMEM((DIRS, n_bl, 2, k, st_loc), f32),
            pltpu.VMEM((stations, 2 * nb), jnp.bfloat16),
            pltpu.VMEM((DIRS, 2, k, nb), f32),
            pltpu.VMEM((n_bl, n_ch, rp, nb_loc), f32),
            pltpu.VMEM((n, rp, nb_loc), f32),
            pltpu.VMEM((rp, nb_loc), f32),
            pltpu.VMEM((n_bl, n_ch, rp, nb_loc), f32),
            pltpu.VMEM((2 * DIRS, nb), f32),
            pltpu.VMEM((n_bl, 2, k, nb_loc), f32),
            pltpu.VMEM((n_bl, 2, k, nb_loc), f32),
            dma((3 + DIRS, n_bl)),
            dma((3 + DIRS, n_bl)),
            dma((n,)),
            dma((n,)),
            dma((n,)),
            dma((n,)),
            dma((n_bl,)),
            dma((n_bl,)),
        ],
        compiler_params=pltpu.CompilerParams(
            collective_id=0, has_side_effects=True, vmem_limit_bytes=VMEM_LIMIT
        ),
        name="peel",
    )(direction_lm, owner, freq, positions, pairs, coh, vis, beams)
    return (res.reshape(2, 1, chans, nb_loc), gains[:, :, None])


def solution(mesh):
    return jax.shard_map(
        functools.partial(on_device, mesh.shape["bl"], mesh.shape["ch"]),
        mesh=mesh,
        in_specs=(
            P(None, "pol", "ch", ("grp", "bl")),
            P("grp", None, "pol", "ch", "bl"),
            P(("grp", "bl"), "pol", "ch"),
            P("grp"),
            P(None, "grp"),
            P("grp", None),
            P(None, ("grp", "bl")),
        ),
        out_specs=(P(None, "pol", "ch", ("grp", "bl")), P("grp", None, "pol", None)),
        check_vma=False,
    )
```

time: 190 us -> 84.3 us (0.44)
  waiting for transfers between devices: 84.1 us -> 0 us
  Pallas kernels: 25.9 us -> 77 us
  blocking collectives: 28.7 us -> 0 us
  starting transfers between devices: 16.9 us -> 0 us
  between operations: 14.2 us -> 0.66 us
  local copies, waits for them, and re-layouts: 16.2 us -> 5.74 us
  other arithmetic: 3.34 us -> 0.67 us
    psum x1 -> x0, waiting for transfers between devices: 69.4 us -> none  [on_device(): sums = lax.psum(sums, ('bl', 'ch'))]
    pallas_call x2 -> x1, Pallas kernels: 25.9 us -> 77 us  [on_device(): pl.pallas_call(functools.partial(one_kernel, n_bl, n_ch), out_shape=(jax....]
    all_gather x1 -> x0, blocking collectives: 28.7 us -> none  [on_device(): all_pairs = lax.all_gather(pairs, 'bl', axis=1, tiled=True)]
    all_to_all x4 -> x0, starting transfers between devices: 16.9 us -> none  [the longest x1 6.32 us: on_device(): lax.all_to_all(coherency[:, 0], 'bl', split_axis=1, concat_axis=0, tiled=...]
    all_to_all x4 -> x0, waiting for transfers between devices: 14.7 us -> none  [the longest x1 6.13 us: on_device(): res = lax.all_to_all(res, 'bl', split_axis=2, concat_axis=1, tiled=True)]
    unnamed x21 -> x18, local copies, waits for them, and re-layouts: 11.2 us -> 5.65 us
    all_to_all x8 -> x0, local copies, waits for them, and re-layouts: 3.7 us -> none  [the longest x2 1.61 us: on_device(): res = lax.all_to_all(res, 'bl', split_axis=2, concat_axis=1, tiled=True)]
  transfers between devices with their start and end apart: 5 -> 0, of which waited for: 4 -> 0; matrix products, arithmetic and copies ran while one was open for 4% -> 0% of each run, Pallas kernels for 0% -> 0%
where the time goes in v2:
time: 84.3 us; the launch traced here: 84.1 us
  Pallas kernels  77 us (91%)
  local copies, waits for them, and re-layouts  5.74 us (7%)
    pallas_call x1, Pallas kernels, on_device(): pl.pallas_call(functools.partial(one_kernel, n_bl, n_ch), out_shape=(jax....  77 us
    unnamed x18, local copies, waits for them, and re-layouts  5.65 us

profile of v2, /device:TPU:0, one launch (start us, length us, event | category | flops | bytes accessed | tf_op | source)
XLA Modules:
  0.0 84.1 jit_solution(8706251565860922289)
XLA Ops:
  0.6 0.0 copy-start.6
  0.6 0.5 broadcast.30
  1.2 0.2 copy-done.6
  1.3 0.7 reduce.3
  2.0 0.1 reshape_squeeze.3
  2.1 0.0 copy-start.5
  2.1 0.7 copy-done.5
  2.8 0.1 copy.18.lm_ref
  2.8 0.0 copy-start.2
  2.8 0.0 copy-start.3
  2.8 0.0 copy-start.4
  2.9 0.7 copy-done.2
  3.5 0.0 copy-done.3
  3.5 0.0 copy-done.4
  3.5 0.0 copy-start
  3.5 1.2 %copy-done = f32[8,2,1,128,128]{4,3,2,1,0:T(8,128)S(1)} copy-done((f32[8,2,1,128,128]{4,3,2,1,0:T(8,128)S(1)}, f32[8,2,1,128,128]{4,3,2,1,0:T(8,128)}, u32[]{:S(2)}) %copy-start) | copy-done | bytes 1048600
  4.8 0.0 copy-start.1
  4.8 0.9 %copy-done.1 = f32[2,1,128,256]{3,2,1,0:T(8,128)S(1)} copy-done((f32[2,1,128,256]{3,2,1,0:T(8,128)S(1)}, f32[2,1,128,256]{3,2,1,0:T(8,128)}, u32[]{:S(2)}) %copy-start.1) | copy-done | bytes 262168
  5.7 77.0 %peel.1 = (f32[2,4,32,256]{3,2,1,0:T(8,128)S(1)}, f32[8,2,512]{2,1,0:T(2,128)S(1)}) custom-call(f32[8,2]{1,0:T(8,128)S(1)} %copy.18.lm_ref, s32[8]{0:T(128)S(1)} %copy-done.4, f32[32,1]{1,0:T(8,128)S(1)} %multiply_add_fusion.freq_ref, f32[2,512]{1,0:T(2,128)S(1)} %copy-done.2, s32[2,256]{1,0:T(2,128)S(1)} %copy-done.3, f32[4,2,32]{2,1,0:T(2,128)S(1)} %bitcast.13, ...), custom_call_target="tpu_custom_call" | custom-call | tf_op jit(solution)/shard_map/peel/pallas_call | solution.py:361
  82.7 0.6 copy.20
  83.4 0.7 copy.24
  (2 shorter events, 0.0 us)
Async XLA Ops:
  0.6 0.7 copy-start.6
  2.1 0.7 copy-start.5
  2.8 0.7 copy-start.2
  2.8 0.7 copy-start.3
  2.8 0.7 copy-start.4
  3.5 1.2 %copy-start = (f32[8,2,1,128,128]{4,3,2,1,0:T(8,128)S(1)}, f32[8,2,1,128,128]{4,3,2,1,0:T(8,128)}, u32[]{:S(2)}) copy-start(f32[8,2,1,128,128]{4,3,2,1,0:T(8,128)} %param.8) | copy-start | bytes 3145732
  4.8 0.9 %copy-start.1 = (f32[2,1,128,256]{3,2,1,0:T(8,128)S(1)}, f32[2,1,128,256]{3,2,1,0:T(8,128)}, u32[]{:S(2)}) copy-start(f32[2,1,128,256]{3,2,1,0:T(8,128)} %param.7) | copy-start | bytes 786436

commit v3 on v2

--- a/solution.py
+++ b/solution.py
@@ -12,6 +12,7 @@
 NC = 256
 DIRS = 8
 MIXING = 0.5
+WINDOW = 4
 VMEM_LIMIT = 48 * 1024 * 1024
 
 
@@ -38,13 +39,6 @@
     rest = turns - jnp.round(turns)
     z = rest * rest
     return horner(COSINE, z), rest * horner(SINE, z)
-
-
-def row_of(d):
-    return 3 * d + d * (d - 1)
-
-
-ROWS = row_of(DIRS)
 
 
 def terms(value, count):
@@ -86,7 +80,6 @@
     nb_loc = pairs_ref.shape[1]
     nb = nb_loc * n_bl
     n = n_bl * n_ch
-    rp = total.shape[0]
     stations = pos_ref.shape[1]
     slot_dev = coh_ref.shape[1]
     my_bl, my_ch = lax.axis_index("bl"), lax.axis_index("ch")
@@ -139,10 +132,14 @@
         )
 
     kinds = 3 + DIRS
-    for kind in range(kinds):
+
+    def send_out(kind):
         for off in range(1, n_bl):
             exchange(kind, lax.rem(my_bl + off, n_bl), my_bl).start()
         own(kind).start()
+
+    for kind in range(3 + WINDOW):
+        send_out(kind)
 
     def arrived(kind):
         own(kind).wait()
@@ -168,22 +165,18 @@
     freq = freq_ref[...]
     eye = lax.broadcasted_iota(jnp.int32, (k, k), 0) == lax.broadcasted_iota(jnp.int32, (k, k), 1)
 
-    def put_row(r, value):
+    def put_row(d, i, value):
         line = jnp.sum(value, axis=0, keepdims=True)
-        c, i = r // rp, r % rp
         for j in range(n_bl):
-            part[j, c, i : i + 1, :] = line[:, j * nb_loc : (j + 1) * nb_loc]
-
-    def get_row(r):
-        c, i = r // rp, r % rp
-        return jnp.concatenate([full[j, c, i : i + 1, :] for j in range(n_bl)], axis=1)
-
-    if n_ch * rp > ROWS:
-        part[...] = jnp.zeros_like(part)
+            part[d][j, i : i + 1, :] = line[:, j * nb_loc : (j + 1) * nb_loc]
+
+    def get_row(d, i):
+        return jnp.concatenate([full[d][j, i : i + 1, :] for j in range(n_bl)], axis=1)
+
     arrived(1)
     arrived(2)
     vis = [jnp.concatenate([vis_in[frm, c] for frm in range(n_bl)], axis=1) for c in range(2)]
-    for d in range(DIRS):
+    def make_model(d):
         turns = freq * (apart[0:1] * lm_ref[d, 0] + apart[1:2] * lm_ref[d, 1])
         cosine, sine = phasor(turns)
         line = jnp.zeros((1, k), jnp.float32)
@@ -194,6 +187,8 @@
         flux = jnp.sum(jnp.where(eye, line, 0.0), axis=1, keepdims=True)
         scale = flux * live
         arrived(3 + d)
+        if d + WINDOW < DIRS:
+            send_out(3 + d + WINDOW)
         e = jnp.concatenate(
             [
                 jnp.concatenate([beam_in[d, frm, c] for frm in range(n_bl)], axis=1)
@@ -210,68 +205,104 @@
         m_i = (cross_r * sine + cross_i * cosine) * scale
         model[d, 0] = m_r
         model[d, 1] = m_i
-        at_row = row_of(d)
-        put_row(at_row, m_r * m_r + m_i * m_i)
-        put_row(at_row + 1, vis[0] * m_r + vis[1] * m_i)
-        put_row(at_row + 2, vis[1] * m_r - vis[0] * m_i)
+        put_row(d, 0, m_r * m_r + m_i * m_i)
+        put_row(d, 1, vis[0] * m_r + vis[1] * m_i)
+        put_row(d, 2, vis[1] * m_r - vis[0] * m_i)
         for f in range(d):
             o_r, o_i = model[f, 0], model[f, 1]
-            put_row(at_row + 3 + 2 * f, o_r * m_r + o_i * m_i)
-            put_row(at_row + 4 + 2 * f, o_i * m_r - o_r * m_i)
-
-    def share(p, slot):
+            put_row(d, 3 + 2 * f, o_r * m_r + o_i * m_i)
+            put_row(d, 4 + 2 * f, o_i * m_r - o_r * m_i)
+
+    def share(d, to_bl):
+        owner = to_bl * n_ch + d % n_ch
+        slot = lax.rem(me - owner + n, n) - 1
         return pltpu.make_async_remote_copy(
-            src_ref=part.at[lax.div(p, n_ch), lax.rem(p, n_ch)],
-            dst_ref=part_in.at[slot],
-            send_sem=sum_send.at[p],
-            recv_sem=sum_recv.at[slot],
+            src_ref=part[d].at[to_bl],
+            dst_ref=part_in[d].at[slot],
+            send_sem=sum_send.at[d],
+            recv_sem=sum_recv.at[d],
+            device_id={"bl": to_bl, "ch": d % n_ch},
+            device_id_type=pl.DeviceIdType.MESH,
+        )
+
+    def spread(d, p):
+        return pltpu.make_async_remote_copy(
+            src_ref=total[d],
+            dst_ref=full[d].at[my_bl],
+            send_sem=all_send.at[d],
+            recv_sem=all_recv.at[d],
             device_id=place(p),
             device_id_type=pl.DeviceIdType.MESH,
         )
 
-    def spread(p, slot):
-        return pltpu.make_async_remote_copy(
-            src_ref=total,
-            dst_ref=full.at[lax.div(slot, n_ch), lax.rem(slot, n_ch)],
-            send_sem=all_send.at[p],
-            recv_sem=all_recv.at[slot],
-            device_id=place(p),
-            device_id_type=pl.DeviceIdType.MESH,
-        )
-
-    def each(body):
-        def step(off, _):
-            body(peer(off))
-            return 0
-
-        lax.fori_loop(1, n, step, 0)
-
-    each(lambda p: share(p, me).start())
-    part_in[me] = part[my_bl, my_ch]
-    each(lambda p: share(p, p).wait_recv())
-    total[...] = lax.fori_loop(1, n, lambda s, acc: acc + part_in[s], part_in[0])
-    each(lambda p: spread(p, me).start())
-    full[my_bl, my_ch] = total[...]
-    each(lambda p: spread(p, p).wait_recv())
-
-    power = jnp.concatenate([get_row(row_of(d)) for d in range(DIRS)], axis=0)
-    weights = add_up(jnp.concatenate([power, power], axis=1), hot[...], 3)
-    for d in range(DIRS):
-        at_row = row_of(d)
-        q, p_r, p_i = get_row(at_row), get_row(at_row + 1), get_row(at_row + 2)
+    def wait_for(ref, count, sem):
+        block = ref.at[pl.ds(0, count)]
+        pltpu.make_async_copy(block, block, sem).wait()
+
+    def start_share(d):
+        for off in range(1, n_bl):
+            share(d, lax.rem(my_bl + off, n_bl)).start()
+
+        @pl.when(my_ch != d % n_ch)
+        def _():
+            share(d, my_bl).start()
+
+    def reduce_and_spread(d):
+        @pl.when(my_ch == d % n_ch)
+        def _():
+            wait_for(part_in[d], n - 1, sum_recv.at[d])
+            value = jnp.sum(part_in[d][...], axis=0) + part[d][my_bl]
+            total[d][...] = value
+
+            def step(off, _):
+                spread(d, peer(off)).start()
+                return 0
+
+            lax.fori_loop(1, n, step, 0)
+            full[d][my_bl] = value
+
+    def sums_arrived(d):
+        @pl.when(my_ch == d % n_ch)
+        def _():
+            if n_bl > 1:
+                wait_for(full[d], n_bl - 1, all_recv.at[d])
+
+        @pl.when(my_ch != d % n_ch)
+        def _():
+            wait_for(full[d], n_bl, all_recv.at[d])
+
+    def sums_sent(d):
+        @pl.when(my_ch == d % n_ch)
+        def _():
+            if n_bl > 1:
+                wait_for(part[d], n_bl - 1, sum_send.at[d])
+            wait_for(part_in[d], n - 1, all_send.at[d])
+
+        @pl.when(my_ch != d % n_ch)
+        def _():
+            wait_for(part[d], n_bl, sum_send.at[d])
+
+    def solve(d):
+        sums_arrived(d)
+        q, p_r, p_i = get_row(d, 0), get_row(d, 1), get_row(d, 2)
         for f in range(d):
-            b_r, b_i = get_row(at_row + 3 + 2 * f), get_row(at_row + 4 + 2 * f)
+            b_r, b_i = get_row(d, 3 + 2 * f), get_row(d, 4 + 2 * f)
             g_r, g_i = pair[2 * f : 2 * f + 1], pair[2 * f + 1 : 2 * f + 2]
             p_r = p_r - (g_r * b_r - g_i * b_i)
             p_i = p_i - (g_r * b_i + g_i * b_r)
-        w = weights[d : d + 1]
         first = add_up(
             jnp.concatenate(
-                [jnp.concatenate([p_r, p_r], axis=1), jnp.concatenate([p_i, -p_i], axis=1)], axis=0
+                [
+                    jnp.concatenate([p_r, p_r], axis=1),
+                    jnp.concatenate([p_i, -p_i], axis=1),
+                    jnp.concatenate([q, q], axis=1),
+                ],
+                axis=0,
             ),
             hot[...],
             3,
         )
+        w = first[2:3]
         scale = 0.5 / (w + MIXING * w + 1.0)
         gain_r = 0.5 + (first[0:1] + MIXING * w + 1.0) * scale
         gain_i = first[1:2] * scale
@@ -296,16 +327,29 @@
         pair[2 * d : 2 * d + 1] = near_r * far_r + near_i * far_i
         pair[2 * d + 1 : 2 * d + 2] = near_i * far_r - near_r * far_i
 
-    for j in range(n_bl):
+    def take_off(j, dirs, r_r, r_i):
         lo, hi = j * nb_loc, (j + 1) * nb_loc
-        r_r, r_i = vis_in[j, 0], vis_in[j, 1]
-        for d in range(DIRS):
+        for d in dirs:
             g_r, g_i = pair[2 * d : 2 * d + 1, lo:hi], pair[2 * d + 1 : 2 * d + 2, lo:hi]
             m_r, m_i = model[d, 0, :, lo:hi], model[d, 1, :, lo:hi]
             r_r = r_r - (g_r * m_r - g_i * m_i)
             r_i = r_i - (g_r * m_i + g_i * m_r)
         res_out[j, 0] = r_r
         res_out[j, 1] = r_i
+
+    for step in range(DIRS + 1):
+        if step < DIRS:
+            make_model(step)
+            start_share(step)
+        if step >= 1:
+            reduce_and_spread(step - 1)
+        if step >= 2:
+            solve(step - 2)
+    for j in range(n_bl):
+        take_off(j, range(DIRS - 1), vis_in[j, 0], vis_in[j, 1])
+    solve(DIRS - 1)
+    for j in range(n_bl):
+        take_off(j, range(DIRS - 1, DIRS), res_out[j, 0], res_out[j, 1])
 
     def back(to, slot):
         return pltpu.make_async_remote_copy(
@@ -331,8 +375,8 @@
         for off in range(1, n_bl):
             to = lax.rem(my_bl + off, n_bl)
             exchange(kind, to, to).wait_send()
-    each(lambda p: share(p, p).wait_send())
-    each(lambda p: spread(p, p).wait_send())
+    for d in range(DIRS):
+        sums_sent(d)
     for off in range(1, n_bl):
         to = lax.rem(my_bl + off, n_bl)
         back(to, to).wait_send()
@@ -347,7 +391,7 @@
     nb = nb_loc * n_bl
     slot_dev = coherency.shape[0]
     n = n_bl * n_ch
-    rp = -(-ROWS // n_ch)
+    rows = [3 + 2 * d for d in range(DIRS)]
     start = lax.axis_index("ch") * chans + lax.axis_index("bl") * k
     freq = 1.0 + 0.5 * (start + jnp.arange(k)).astype(jnp.float32)[:, None] / NC
     coh = coherency[:, 0].reshape(slot_dev, n_bl, k).transpose(1, 0, 2)
@@ -373,19 +417,19 @@
             pltpu.VMEM((DIRS, n_bl, 2, k, st_loc), f32),
             pltpu.VMEM((stations, 2 * nb), jnp.bfloat16),
             pltpu.VMEM((DIRS, 2, k, nb), f32),
-            pltpu.VMEM((n_bl, n_ch, rp, nb_loc), f32),
-            pltpu.VMEM((n, rp, nb_loc), f32),
-            pltpu.VMEM((rp, nb_loc), f32),
-            pltpu.VMEM((n_bl, n_ch, rp, nb_loc), f32),
+            [pltpu.VMEM((n_bl, r, nb_loc), f32) for r in rows],
+            [pltpu.VMEM((n - 1, r, nb_loc), f32) for r in rows],
+            [pltpu.VMEM((r, nb_loc), f32) for r in rows],
+            [pltpu.VMEM((n_bl, r, nb_loc), f32) for r in rows],
             pltpu.VMEM((2 * DIRS, nb), f32),
             pltpu.VMEM((n_bl, 2, k, nb_loc), f32),
             pltpu.VMEM((n_bl, 2, k, nb_loc), f32),
             dma((3 + DIRS, n_bl)),
             dma((3 + DIRS, n_bl)),
-            dma((n,)),
-            dma((n,)),
-            dma((n,)),
-            dma((n,)),
+            dma((DIRS,)),
+            dma((DIRS,)),
+            dma((DIRS,)),
+            dma((DIRS,)),
             dma((n_bl,)),
             dma((n_bl,)),
         ],

time: 84.3 us -> 82 us (0.973)
  Pallas kernels: 77 us -> 74.6 us
    pallas_call x1, Pallas kernels: 77 us -> 74.6 us  [on_device(): pl.pallas_call(functools.partial(one_kernel, n_bl, n_ch), out_shape=(jax....]
where the time goes in v3:
time: 82 us; the launch traced here: 81.7 us
  Pallas kernels  74.6 us (91%)
  local copies, waits for them, and re-layouts  5.74 us (7%)
    pallas_call x1, Pallas kernels, on_device(): pl.pallas_call(functools.partial(one_kernel, n_bl, n_ch), out_shape=(jax....  74.6 us
    unnamed x18, local copies, waits for them, and re-layouts  5.65 us

profile of v3, /device:TPU:0, one launch (start us, length us, event | category | flops | bytes accessed | tf_op | source)
XLA Modules:
  0.0 81.7 jit_solution(10032517213157991488)
XLA Ops:
  0.6 0.0 copy-start.6
  0.6 0.5 broadcast.30
  1.2 0.2 copy-done.6
  1.3 0.7 reduce.3
  2.0 0.1 reshape_squeeze.3
  2.1 0.0 copy-start.5
  2.1 0.7 copy-done.5
  2.8 0.1 copy.18.lm_ref
  2.8 0.0 copy-start.2
  2.8 0.0 copy-start.3
  2.8 0.0 copy-start.4
  2.9 0.7 copy-done.2
  3.5 0.0 copy-done.3
  3.5 0.0 copy-done.4
  3.5 0.0 copy-start
  3.5 1.2 %copy-done = f32[8,2,1,128,128]{4,3,2,1,0:T(8,128)S(1)} copy-done((f32[8,2,1,128,128]{4,3,2,1,0:T(8,128)S(1)}, f32[8,2,1,128,128]{4,3,2,1,0:T(8,128)}, u32[]{:S(2)}) %copy-start) | copy-done | bytes 1048600
  4.8 0.0 copy-start.1
  4.8 0.9 %copy-done.1 = f32[2,1,128,256]{3,2,1,0:T(8,128)S(1)} copy-done((f32[2,1,128,256]{3,2,1,0:T(8,128)S(1)}, f32[2,1,128,256]{3,2,1,0:T(8,128)}, u32[]{:S(2)}) %copy-start.1) | copy-done | bytes 262168
  5.7 74.6 %peel.1 = (f32[2,4,32,256]{3,2,1,0:T(8,128)S(1)}, f32[8,2,512]{2,1,0:T(2,128)S(1)}) custom-call(f32[8,2]{1,0:T(8,128)S(1)} %copy.18.lm_ref, s32[8]{0:T(128)S(1)} %copy-done.4, f32[32,1]{1,0:T(8,128)S(1)} %multiply_add_fusion.freq_ref, f32[2,512]{1,0:T(2,128)S(1)} %copy-done.2, s32[2,256]{1,0:T(2,128)S(1)} %copy-done.3, f32[4,2,32]{2,1,0:T(2,128)S(1)} %bitcast.13, ...), custom_call_target="tpu_custom_call" | custom-call | tf_op jit(solution)/shard_map/peel/pallas_call | solution.py:405
  80.4 0.6 copy.20
  81.0 0.7 copy.24
  (2 shorter events, 0.0 us)
Async XLA Ops:
  0.6 0.7 copy-start.6
  2.1 0.7 copy-start.5
  2.8 0.7 copy-start.2
  2.8 0.7 copy-start.3
  2.8 0.7 copy-start.4
  3.5 1.2 %copy-start = (f32[8,2,1,128,128]{4,3,2,1,0:T(8,128)S(1)}, f32[8,2,1,128,128]{4,3,2,1,0:T(8,128)}, u32[]{:S(2)}) copy-start(f32[8,2,1,128,128]{4,3,2,1,0:T(8,128)} %param.8) | copy-start | bytes 3145732
  4.8 0.9 %copy-start.1 = (f32[2,1,128,256]{3,2,1,0:T(8,128)S(1)}, f32[2,1,128,256]{3,2,1,0:T(8,128)}, u32[]{:S(2)}) copy-start(f32[2,1,128,256]{3,2,1,0:T(8,128)} %param.7) | copy-start | bytes 786436

commit v4 on v3

--- a/solution.py
+++ b/solution.py
@@ -13,6 +13,7 @@
 DIRS = 8
 MIXING = 0.5
 WINDOW = 4
+LAG = 4
 VMEM_LIMIT = 48 * 1024 * 1024
 
 
@@ -337,14 +338,14 @@
         res_out[j, 0] = r_r
         res_out[j, 1] = r_i
 
-    for step in range(DIRS + 1):
+    for step in range(DIRS - 1 + LAG):
         if step < DIRS:
             make_model(step)
             start_share(step)
-        if step >= 1:
+        if step >= LAG:
+            solve(step - LAG)
+        if 1 <= step <= DIRS:
             reduce_and_spread(step - 1)
-        if step >= 2:
-            solve(step - 2)
     for j in range(n_bl):
         take_off(j, range(DIRS - 1), vis_in[j, 0], vis_in[j, 1])
     solve(DIRS - 1)

time: 82 us -> 76.3 us (0.930)
  Pallas kernels: 74.6 us -> 69 us
    pallas_call x1, Pallas kernels: 74.6 us -> 69 us  [on_device(): pl.pallas_call(functools.partial(one_kernel, n_bl, n_ch), out_shape=(jax....]
where the time goes in v4:
time: 76.3 us; the launch traced here: 76 us
  Pallas kernels  69 us (90%)
  local copies, waits for them, and re-layouts  5.74 us (8%)
    pallas_call x1, Pallas kernels, on_device(): pl.pallas_call(functools.partial(one_kernel, n_bl, n_ch), out_shape=(jax....  69 us
    unnamed x18, local copies, waits for them, and re-layouts  5.65 us

profile of v4, /device:TPU:0, one launch (start us, length us, event | category | flops | bytes accessed | tf_op | source)
XLA Modules:
  0.0 76.0 jit_solution(3926729127248189203)
XLA Ops:
  0.6 0.0 copy-start.6
  0.6 0.5 broadcast.30
  1.2 0.2 copy-done.6
  1.3 0.7 reduce.3
  2.0 0.1 reshape_squeeze.3
  2.1 0.0 copy-start.5
  2.1 0.7 copy-done.5
  2.8 0.1 copy.18.lm_ref
  2.8 0.0 copy-start.2
  2.8 0.0 copy-start.3
  2.8 0.0 copy-start.4
  2.9 0.7 copy-done.2
  3.5 0.0 copy-done.3
  3.5 0.0 copy-done.4
  3.5 0.0 copy-start
  3.5 1.2 %copy-done = f32[8,2,1,128,128]{4,3,2,1,0:T(8,128)S(1)} copy-done((f32[8,2,1,128,128]{4,3,2,1,0:T(8,128)S(1)}, f32[8,2,1,128,128]{4,3,2,1,0:T(8,128)}, u32[]{:S(2)}) %copy-start) | copy-done | bytes 1048600
  4.8 0.0 copy-start.1
  4.8 0.9 %copy-done.1 = f32[2,1,128,256]{3,2,1,0:T(8,128)S(1)} copy-done((f32[2,1,128,256]{3,2,1,0:T(8,128)S(1)}, f32[2,1,128,256]{3,2,1,0:T(8,128)}, u32[]{:S(2)}) %copy-start.1) | copy-done | bytes 262168
  5.7 69.0 %peel.1 = (f32[2,4,32,256]{3,2,1,0:T(8,128)S(1)}, f32[8,2,512]{2,1,0:T(2,128)S(1)}) custom-call(f32[8,2]{1,0:T(8,128)S(1)} %copy.18.lm_ref, s32[8]{0:T(128)S(1)} %copy-done.4, f32[32,1]{1,0:T(8,128)S(1)} %multiply_add_fusion.freq_ref, f32[2,512]{1,0:T(2,128)S(1)} %copy-done.2, s32[2,256]{1,0:T(2,128)S(1)} %copy-done.3, f32[4,2,32]{2,1,0:T(2,128)S(1)} %bitcast.13, ...), custom_call_target="tpu_custom_call" | custom-call | tf_op jit(solution)/shard_map/peel/pallas_call | solution.py:406
  74.7 0.6 copy.20
  75.3 0.7 copy.24
  (2 shorter events, 0.0 us)
Async XLA Ops:
  0.6 0.7 copy-start.6
  2.1 0.7 copy-start.5
  2.8 0.7 copy-start.2
  2.8 0.7 copy-start.3
  2.8 0.7 copy-start.4
  3.5 1.2 %copy-start = (f32[8,2,1,128,128]{4,3,2,1,0:T(8,128)S(1)}, f32[8,2,1,128,128]{4,3,2,1,0:T(8,128)}, u32[]{:S(2)}) copy-start(f32[8,2,1,128,128]{4,3,2,1,0:T(8,128)} %param.8) | copy-start | bytes 3145732
  4.8 0.9 %copy-start.1 = (f32[2,1,128,256]{3,2,1,0:T(8,128)S(1)}, f32[2,1,128,256]{3,2,1,0:T(8,128)}, u32[]{:S(2)}) copy-start(f32[2,1,128,256]{3,2,1,0:T(8,128)} %param.7) | copy-start | bytes 786436
